TPU v7x, 256 devices: a whole 4x4x8 slice. The times are simulated.
256 devices in a mesh: layer: 2 (over core), row: 16 (over z, y_lo), col: 8 (over x, y_hi).
Axes of the slice: x: 4, y: 4 (y_hi: 2, y_lo: 2; y = y_hi * 2 + y_lo), z: 8, core: 2. Of those that a mesh axis runs over, the one named last changes fastest.
Arguments:
- left_tensor: float32 [2048, 8192], P('row', ('layer', 'col')), may hold values from -6 to 6
- right_tensor: float32 [8192, 8192], P(('layer', 'row'), 'col'), may hold values from -0.5 to 0.5
- left_occupied: int32 [32, 128], replicated, may hold values from 0 to 1, as said below
- right_occupied: int32 [128, 128], replicated, may hold values from 0 to 1, as said below
Outputs:
- polarizability: float32 [2048, 8192], P('row', 'col')
Inputs may be any that keep to these rules, and one draw needn't show every extreme that they name: `left_occupied`: block occupancy flags. Each device's share of left_tensor (2 x 8 blocks) has at most 3 occupied blocks, and some share has exactly 3. `right_occupied`: block occupancy flags. Each device's share of right_tensor (4 x 16 blocks) has at most 12 occupied blocks, and some share has exactly 12.
All inputs are finite; a program needn't handle non-finite values.
Results may differ from a plain program's by a relative error of at most 0.000071.
Values sent between devices are 32-bit elements; how exact they have to be, the bound alone decides.
No kernel may reach another device: no remote copies, remote signals or barrier semaphores. Data moves between devices by JAX's collectives and lax.ppermute only.
A program may use at most 192 MiB of HBM per device.

v0:
```python
import functools

import jax
import jax.numpy as jnp
from jax import lax
from jax.experimental import pallas as pl
from jax.experimental.pallas import tpu as pltpu
from jax.sharding import PartitionSpec as P


BLK = 64
KB = 4
JB = 16
LI, LQ = 2, 8
RCAP, LCAP = 12, 3
NZ, NC = 8, 8
SHARE = KB * BLK
COLS = JB * BLK
ROWS = 2 * LI * BLK
SLABS = RCAP // 2
LPACK = 96
F32, BF16 = jnp.float32, jnp.bfloat16
VMEM = pl.BlockSpec(memory_space=pltpu.VMEM)
SMEM = pl.BlockSpec(memory_space=pltpu.SMEM)
HBM = pl.BlockSpec(memory_space=pltpu.HBM)
PARAMS = pltpu.CompilerParams(vmem_limit_bytes=32 * 1024 * 1024)
EMPTY = RCAP
HELD = (SLABS + 1) * BLK


def place():
    r = lax.axis_index("row")
    return lax.axis_index("layer"), r // 2, r % 2, lax.axis_index("col")


def low_half(shape):
    return lax.broadcasted_iota(jnp.int32, shape, 1) < BLK


def cost(flops, moved):
    return pl.CostEstimate(flops=flops, bytes_accessed=moved, transcendentals=0)


def block_at(ref, e, per_row, odd):
    k, j = e // per_row, e % per_row
    v = ref[
        pl.ds(pl.multiple_of(k * BLK, BLK), BLK),
        pl.ds(pl.multiple_of((j // 2) * 128, 128), 128),
    ]
    return jnp.where(j % 2 == odd, v, pltpu.roll(v, BLK, 1))


def ranks(flags, per_row, rows, none):
    n = flags.shape[0]
    f = flags.astype(F32)
    a, b = grid((128, 128))
    same = a // per_row == b // per_row
    in_row = pick(f, same & (a < b))
    row_sum = pick(f, same)
    a, b = grid((n, n))
    before = pick((a // rows == b // rows) & (b < a), row_sum)
    return jnp.where(f > 0, in_row + before, none)


def grid(shape):
    return [lax.broadcasted_iota(jnp.int32, shape, d) for d in (0, 1)]


def pick(a, b):
    return jnp.dot(
        a.astype(F32).astype(BF16), b.astype(F32).astype(BF16), preferred_element_type=F32
    )


def pack(
    left_hbm, right_hbm, left_occupied, right_occupied, left_out, right_out,
    left, right, lflags, rflags, lindex, rindex, sems,
):
    l, z, y, c = place()
    ltop = pl.multiple_of((z // 2) * 8, 8)
    rtop = pl.multiple_of(l * 64 + z * 8, 8)
    copies = [
        pltpu.make_async_copy(right_occupied.at[pl.ds(rtop, 8)], rflags, sems.at[0]),
        pltpu.make_async_copy(left_occupied.at[pl.ds(ltop, 8)], lflags, sems.at[1]),
        pltpu.make_async_copy(right_hbm, right, sems.at[2]),
        pltpu.make_async_copy(left_hbm, left, sems.at[3]),
    ]
    for copy in copies:
        copy.start()
    copies[0].wait()
    rcount = jnp.int32(0)
    for k in range(KB):
        for j in range(JB):
            rindex[rcount] = k * JB + j
            rcount += rflags[y * KB + k, c * JB + j]
    copies[1].wait()
    lcount = jnp.int32(0)
    for i in range(LI):
        for q in range(LQ):
            lindex[lcount] = i * LQ + q
            lcount += lflags[(z % 2) * 4 + y * LI + i, l * 64 + c * LQ + q]
    low = low_half((BLK, 128))
    copies[2].wait()
    for p in range(SLABS):
        ea = jnp.where(2 * p < rcount, rindex[2 * p], 0)
        eb = jnp.where(2 * p + 1 < rcount, rindex[2 * p + 1], 0)
        right_out[p * BLK : (p + 1) * BLK, :] = jnp.where(
            low, block_at(right, ea, JB, 0), block_at(right, eb, JB, 1)
        )
    copies[3].wait()
    e = [jnp.where(s < lcount, lindex[s], 0) for s in range(LCAP)]
    left_out[:BLK, :] = jnp.where(low, block_at(left, e[0], LQ, 0), block_at(left, e[1], LQ, 1))
    a = block_at(left, e[2], LQ, 0)
    b = block_at(left, e[2], LQ, 1)
    left_out[BLK:, :] = jnp.where(low_half((BLK // 2, 128)), a[: BLK // 2], b[BLK // 2 :])


def tables(left_occupied, right_occupied, slots, lall, rall, sems):
    l, z, y, c = place()
    ltop = pl.multiple_of((z // 2) * 8, 8)
    ptop = pl.multiple_of(l * 64, 64)
    copies = [
        pltpu.make_async_copy(right_occupied.at[pl.ds(ptop, 64)], rall, sems.at[0]),
        pltpu.make_async_copy(left_occupied.at[pl.ds(ltop, 8)], lall, sems.at[1]),
    ]
    for copy in copies:
        copy.start()
    for copy in copies:
        copy.wait()
    rank = ranks(rall[...], JB, KB, float(EMPTY))
    a, b = grid((8, 64))
    g, h = grid((128, 128))
    total = jnp.zeros((8, 128), F32)
    for k in range(KB):
        row = pick(b == a * 8 + y * KB + k, rank)
        total += pick(row, (h // JB == k) & (g == c * JB + h % JB))
    slots[:8, :] = total.astype(jnp.int32)
    rank = ranks(lall[...], LQ, LI, -1.0)
    a, b = grid((8, 8))
    row = pick(b == (z % 2) * 4 + a, rank)
    row = pick(row, (h < 32) & (g == l * 64 + (h // KB) * LQ + y * KB + h % KB))
    slots[8:, :] = row.astype(jnp.int32)


def join(*refs):
    *parts, out = refs
    for t, part in enumerate(parts):
        out[t * LPACK : (t + 1) * LPACK, :] = part[...]


def split(v):
    h = v.astype(BF16)
    return h, (v - h.astype(F32)).astype(BF16)


def unpack_left(mine, index, a0, a1, a2, a3, out):
    l, z, y, c = place()
    x = c // 2
    low = low_half((BLK, 128))
    low2 = low_half((BLK // 2, 128))
    for d, ref in enumerate((a0, a1, a2, a3)):
        for part in (0, 2) if mine else (1, 3):
            yh = (c % 2) ^ (part // 2)
            yl = y ^ (part % 2)
            column = ((x + d) % 4) * 2 + yh
            base = part * LPACK
            v = ref[base : base + BLK, :]
            w = ref[base + BLK : base + LPACK, :]
            vr, wr = pltpu.roll(v, BLK, 1), pltpu.roll(w, BLK, 1)
            s0 = jnp.where(low, v, vr)
            s1 = jnp.where(low, vr, v)
            s2 = jnp.concatenate([jnp.where(low2, w, wr), jnp.where(low2, wr, w)], axis=0)
            for i in range(LI):
                for p in range(KB // 2):
                    at = column * KB + 2 * p
                    slot = jnp.where(low, index[8 + yl * LI + i, at], index[8 + yl * LI + i, at + 1])
                    t = jnp.where(slot == 0, s0, jnp.where(slot == 1, s1, jnp.where(slot == 2, s2, 0.0)))
                    lanes = pl.ds(pl.multiple_of(column * SHARE + p * 128, 128), 128)
                    h, g = split(t)
                    out[i * BLK : (i + 1) * BLK, lanes] = h
                    out[128 + i * BLK : 128 + (i + 1) * BLK, lanes] = g


def spread(index, source, pieces, two, hi, lo, first=0):
    low = low_half((BLK, 128))
    top = 0
    for piece in pieces:
        v = piece[...]
        n = v.shape[0]
        two[top : top + n, :] = v
        two[HELD + top : HELD + top + n, :] = pltpu.roll(v, BLK, 1)
        top += n
    two[SLABS * BLK : HELD, :] = jnp.zeros((BLK, 128), F32)
    two[HELD + SLABS * BLK :, :] = jnp.zeros((BLK, 128), F32)
    for k in range(KB):
        for p in range(hi.shape[1] // 128):
            s0 = index[source, k * JB + 2 * (first + p)]
            s1 = index[source, k * JB + 2 * (first + p) + 1]
            r0 = (s0 & 1) * HELD + lax.shift_right_logical(s0, 1) * BLK
            r1 = (1 - (s1 & 1)) * HELD + lax.shift_right_logical(s1, 1) * BLK
            v0 = two[pl.ds(pl.multiple_of(r0, BLK), BLK), :]
            v1 = two[pl.ds(pl.multiple_of(r1, BLK), BLK), :]
            h, g = split(jnp.where(low, v0, v1))
            hi[k * BLK : (k + 1) * BLK, p * 128 : (p + 1) * 128] = h
            lo[k * BLK : (k + 1) * BLK, p * 128 : (p + 1) * 128] = g


def unpack_right(offsets, index, *refs):
    n = len(offsets)
    shares, (hi, lo, two) = refs[:n], refs[n:]
    l, z, y, c = place()
    for t, offset in enumerate(offsets):
        spread(index, (z + offset) % NZ, shares[t : t + 1], two.at[t], hi.at[t], lo.at[t])


def product(left, ks, hi, lo):
    dot = functools.partial(jnp.dot, preferred_element_type=F32)
    big = dot(left[:, ks], hi)
    return (big[128:] + dot(left[:128, ks], lo)) + big[:128]


def finish(offset, keep, index, left, share0, share1, total, out, two, hi, lo):
    l, z, y, c = place()
    source = (z + offset) % NZ
    half = l if keep else 1 - l
    spread(index, source, (share0, share1), two, hi, lo, half * (JB // 4))
    ks = pl.ds(pl.multiple_of(source * SHARE, SHARE), SHARE)
    width = COLS // 2
    for n0 in range(0, width, 256):
        cols = pl.ds(pl.multiple_of(half * width + n0, 256), 256)
        out[:, n0 : n0 + 256] = total[:, cols] + product(
            left, ks, hi[:, n0 : n0 + 256], lo[:, n0 : n0 + 256]
        )


def multiply(ready, fresh, index, left, *refs):
    refs = list(refs)
    take = lambda n: [refs.pop(0) for _ in range(n)]
    l, z, y, c = place()
    parts = []
    for group in ready:
        hi, lo = take(2)
        parts += [(offset, hi.at[t], lo.at[t]) for t, offset in enumerate(group)]
    shares = [take(n) for _, n in fresh]
    out, two, hi, lo = refs
    for t, (offset, _) in enumerate(fresh):
        spread(index, (z + offset) % NZ, shares[t], two.at[t], hi.at[t], lo.at[t])
        parts.append((offset, hi.at[t], lo.at[t]))
    for n0 in range(0, COLS, 256):
        cols = slice(n0, n0 + 256)
        done = None
        for offset, h, g in parts:
            ks = pl.ds(pl.multiple_of(((z + offset) % NZ) * SHARE, SHARE), SHARE)
            one = product(left, ks, h[:, cols], g[:, cols])
            done = one if done is None else done + one
        out[:, cols] = done


def in_hbm(arrays):
    return [pltpu.with_memory_space_constraint(a, pltpu.HBM) for a in arrays]


def call_pack(*args):
    return pl.pallas_call(
        pack,
        out_shape=(
            jax.ShapeDtypeStruct((LPACK, 128), F32),
            jax.ShapeDtypeStruct((SLABS * BLK, 128), F32),
        ),
        in_specs=[HBM] * 4,
        out_specs=(VMEM, VMEM),
        scratch_shapes=[
            pltpu.VMEM((LI * BLK, LQ * BLK), F32),
            pltpu.VMEM((SHARE, COLS), F32),
            pltpu.SMEM((8, 128), jnp.int32),
            pltpu.SMEM((8, 128), jnp.int32),
            pltpu.SMEM((16,), jnp.int32),
            pltpu.SMEM((16,), jnp.int32),
            pltpu.SemaphoreType.DMA((4,)),
        ],
        compiler_params=PARAMS,
        cost_estimate=cost(0, 1 << 20),
    )(*in_hbm(args))


def call_tables(*args):
    return pl.pallas_call(
        tables,
        out_shape=jax.ShapeDtypeStruct((16, 128), jnp.int32),
        in_specs=[HBM] * 2,
        out_specs=VMEM,
        scratch_shapes=[
            pltpu.VMEM((8, 128), jnp.int32),
            pltpu.VMEM((64, 128), jnp.int32),
            pltpu.SemaphoreType.DMA((2,)),
        ],
        compiler_params=PARAMS,
        cost_estimate=cost(0, 1 << 18),
    )(*in_hbm(args))


def call_join(parts):
    return pl.pallas_call(
        join,
        out_shape=jax.ShapeDtypeStruct((len(parts) * LPACK, 128), F32),
        in_specs=[VMEM] * len(parts),
        out_specs=VMEM,
        compiler_params=PARAMS,
        cost_estimate=cost(0, 1 << 18),
    )(*parts)


def call_unpack_left(mine, index, lefts):
    return pl.pallas_call(
        functools.partial(unpack_left, mine),
        out_shape=jax.ShapeDtypeStruct((256, NZ * SHARE), BF16),
        in_specs=[SMEM] + [VMEM] * 4,
        out_specs=VMEM,
        compiler_params=PARAMS,
        cost_estimate=cost(0, 1 << 16),
    )(index, *lefts)


def call_unpack_right(offsets, index, shares):
    n = len(offsets)
    return pl.pallas_call(
        functools.partial(unpack_right, offsets),
        out_shape=(jax.ShapeDtypeStruct((n, SHARE, COLS), BF16),) * 2,
        in_specs=[SMEM] + [VMEM] * n,
        out_specs=(VMEM, VMEM),
        scratch_shapes=[pltpu.VMEM((n, 2 * HELD, 128), F32)],
        compiler_params=PARAMS,
        cost_estimate=cost(0, n << 20),
    )(index, *shares)


def call_multiply(index, left, ready, fresh):
    n = len(fresh)
    operands = [array for _, arrays in ready for array in arrays]
    operands += [piece for _, pieces in fresh for piece in pieces]
    count = n + sum(len(offsets) for offsets, _ in ready)
    kernel = functools.partial(
        multiply,
        [offsets for offsets, _ in ready],
        [(offset, len(pieces)) for offset, pieces in fresh],
    )
    return pl.pallas_call(
        kernel,
        out_shape=jax.ShapeDtypeStruct((128, COLS), F32),
        in_specs=[SMEM] + [VMEM] * (1 + len(operands)),
        out_specs=VMEM,
        scratch_shapes=[
            pltpu.VMEM((n, 2 * HELD, 128), F32),
            pltpu.VMEM((n, SHARE, COLS), BF16),
            pltpu.VMEM((n, SHARE, COLS), BF16),
        ],
        compiler_params=PARAMS,
        cost_estimate=cost(count * 3 * ROWS * SHARE * COLS, 4 * ROWS * COLS),
    )(index, left, *operands)


def call_finish(offset, keep, index, left, pieces, total):
    width = COLS // 2
    return pl.pallas_call(
        functools.partial(finish, offset, keep),
        out_shape=jax.ShapeDtypeStruct((128, width), F32),
        in_specs=[SMEM] + [VMEM] * 4,
        out_specs=VMEM,
        scratch_shapes=[
            pltpu.VMEM((2 * HELD, 128), F32),
            pltpu.VMEM((SHARE, width), BF16),
            pltpu.VMEM((SHARE, width), BF16),
        ],
        compiler_params=PARAMS,
        cost_estimate=cost(3 * 128 * SHARE * COLS, ROWS * COLS),
    )(index, left, *pieces, total)


def assemble(mine, theirs, other, rest, out):
    l = lax.axis_index("layer")
    width = COLS // 2
    for half, part in ((l, other), (1 - l, rest)):
        cols = pl.ds(pl.multiple_of(half * width, width), width)
        out[:, cols] = mine[:, cols] + theirs[:, cols] + part[...]


def call_assemble(*args):
    return pl.pallas_call(
        assemble,
        out_shape=jax.ShapeDtypeStruct((128, COLS), F32),
        in_specs=[VMEM] * 4,
        out_specs=VMEM,
        compiler_params=PARAMS,
        cost_estimate=cost(0, 1 << 21),
    )(*args)


def z_perm(d):
    return [(z * 2 + y, ((z + d) % NZ) * 2 + y) for z in range(NZ) for y in range(2)]


def x_perm(d):
    return [(((x + d) % 4) * 2 + y, x * 2 + y) for x in range(4) for y in range(2)]


def local(left_tensor, right_tensor, left_occupied, right_occupied):
    left0, right0 = call_pack(left_tensor, right_tensor, left_occupied, right_occupied)
    index = call_tables(left_occupied, right_occupied)

    pair = [(r, r ^ 1) for r in range(16)]
    near = lambda dy, dh: [(r * 8 + c, (r ^ dy) * 8 + (c ^ dh)) for r in range(16) for c in range(8)]
    z_send = lambda v, d: lax.ppermute(v, "row", z_perm(d))
    up1, down1 = z_send(right0, 1), z_send(right0, -1)
    nears = [lax.ppermute(left0, ("row", "col"), near(dy, dh)) for dy, dh in ((1, 0), (0, 1), (1, 1))]
    rights0 = call_unpack_right((0,), index, (right0,))
    up1, down1, rights0, *nears = lax.optimization_barrier((up1, down1, rights0, *nears))
    left2 = call_join([left0] + nears)
    up2, down2 = z_send(up1, 1), z_send(down1, -1)
    x_send = lambda v, d: lax.ppermute(v, "col", x_perm(d))
    lefts = [left2] + [x_send(left2, d) for d in (1, 2, 3)]
    up3, down3 = z_send(up2, 1), z_send(down2, -1)
    near_z = (-1, 1, -2, 2)
    rights = call_unpack_right(near_z, index, (up1, down1, up2, down2))
    ready = [((0,), rights0), (near_z, rights)]
    third = [(-3, (up3,)), (3, (down3,))]
    half = SLABS * BLK // 2
    far = z_send(up3[:half], 1), z_send(down3[half:], -1)

    left = call_unpack_left(False, index, lefts)
    swap = [(0, 1), (1, 0)]
    total = call_multiply(index, left, ready, third)
    give = call_finish(4, False, index, left, far, total)
    recv = lax.ppermute(give, "layer", swap)
    keep = call_finish(4, True, index, left, far, total)
    send = keep + recv
    other = lax.ppermute(send, "row", pair)
    index, send = lax.optimization_barrier((index, send))
    own = call_unpack_left(True, index, lefts)
    mine = call_multiply(index, own, ready, third + [(4, far)])
    theirs = lax.ppermute(mine, "layer", swap)
    rest = lax.ppermute(other, "layer", swap)
    return call_assemble(mine, theirs, other, rest)


def solution(mesh):
    placed = (P("row", ("layer", "col")), P(("layer", "row"), "col"), P(), P())
    return jax.shard_map(
        local, mesh=mesh, in_specs=placed, out_specs=P("row", "col"), check_vma=False
    )
```

profile of v0, /device:TPU:1, one launch (start us, length us, event | category | flops | bytes accessed | tf_op | source)
XLA Modules:
  0.0 53.4 jit_solution(4397753534998858516)
XLA Ops:
  0.0 1.6 %shard_map.47 = (f32[96,128]{1,0:T(8,128)S(1)}, f32[384,128]{1,0:T(8,128)S(1)}) custom-call(f32[128,512]{1,0:T(8,128)} %left_hbm.1, f32[256,1024]{1,0:T(8,128)} %right_hbm.1, s32[32,128]{1,0:T(8,128)} %left_occupied.3, s32[128,128]{1,0:T(8,128)} %right_occupied.3), custom_call_target="tpu_custom_call" | custom-call | bytes 1048576 | tf_op jit(solution)/shard_map/pallas_call | solution.py:264
  1.6 6.5 %collective-permute-start.1 = (f32[384,128]{1,0:T(8,128)S(1)}, f32[384,128]{1,0:T(8,128)S(1)}, u32[]{:S(2)}, u32[]{:S(2)}) collective-permute-start(f32[384,128]{1,0:T(8,128)S(1)} %get-tuple-element.20.refs_0_), channel_id=1, source_target_pairs={{0,112},{8,120},{16,0},{24,8},{32,16},{40,24},{48,32},{56,40},{64,... | collective-permute-start | bytes 589832 | tf_op jit(solution)/shard_map/ppermute | solution.py:412
  8.1 2.7 %collective-permute-start.4 = (f32[96,128]{1,0:T(8,128)S(1)}, f32[96,128]{1,0:T(8,128)S(1)}, u32[]{:S(2)}, u32[]{:S(2)}) collective-permute-start(f32[96,128]{1,0:T(8,128)S(1)} %get-tuple-element.19.refs_0_), channel_id=1, source_target_pairs={{0,9},{1,8},{2,11},{3,10},{4,13},{5,12},{6,15},{7,14},{8,1},{9,0},... | collective-permute-start | bytes 147464 | tf_op jit(solution)/shard_map/ppermute | solution.py:414
  11.4 1.6 %shard_map.46.index = s32[16,128]{1,0:T(8,128)S(1)} custom-call(s32[32,128]{1,0:T(8,128)} %left_occupied.3, s32[128,128]{1,0:T(8,128)} %right_occupied.3), custom_call_target="tpu_custom_call" | custom-call | bytes 262144 | tf_op jit(solution)/shard_map/pallas_call | solution.py:287
  13.0 1.1 %shard_map.48 = (bf16[1,256,1024]{2,1,0:T(8,128)(2,1)S(1)}, bf16[1,256,1024]{2,1,0:T(8,128)(2,1)S(1)}) custom-call(s32[16,128]{1,0:T(8,128)S(1)} %shard_map.46.index, f32[384,128]{1,0:T(8,128)S(1)} %get-tuple-element.20.refs_0_), custom_call_target="tpu_custom_call" | custom-call | bytes 1048576 | tf_op jit(solution)/shard_map/pallas_call | solution.py:326
  14.1 1.2 %collective-permute-done.3.refs_2_ = f32[96,128]{1,0:T(8,128)S(1)} collective-permute-done((f32[96,128]{1,0:T(8,128)S(1)}, f32[96,128]{1,0:T(8,128)S(1)}, u32[]{:S(2)}, u32[]{:S(2)}) %collective-permute-start.3) | collective-permute-done | bytes 49184 | tf_op jit(solution)/shard_map/ppermute | solution.py:414
  15.4 2.7 %collective-permute-start.11 = (f32[384,128]{1,0:T(8,128)S(1)}, f32[384,128]{1,0:T(8,128)S(1)}, u32[]{:S(2)}, u32[]{:S(2)}) collective-permute-start(f32[384,128]{1,0:T(8,128)S(1)} %collective-permute-done.1.refs_1_), channel_id=1, source_target_pairs={{0,112},{8,120},{16,0},{24,8},{32,16},{40,24},{48,32},{56,40},{64,... | collective-permute-start | bytes 589832 | tf_op jit(solution)/shard_map/ppermute | solution.py:412
  18.1 1.3 %collective-permute-start.7 = (f32[384,128]{1,0:T(8,128)S(1)}, f32[384,128]{1,0:T(8,128)S(1)}, u32[]{:S(2)}, u32[]{:S(2)}) collective-permute-start(f32[384,128]{1,0:T(8,128)S(1)} %shard_map.49.a0), channel_id=1, source_target_pairs={{6,0},{7,1},{0,2},{1,3},{2,4},{3,5},{4,6},{5,7},{14,8},{15,9},{8,1... | collective-permute-start | bytes 589832 | tf_op jit(solution)/shard_map/ppermute | solution.py:419
  19.4 2.5 %collective-permute-start.6 = (f32[384,128]{1,0:T(8,128)S(1)}, f32[384,128]{1,0:T(8,128)S(1)}, u32[]{:S(2)}, u32[]{:S(2)}) collective-permute-start(f32[384,128]{1,0:T(8,128)S(1)} %shard_map.49.a0), channel_id=1, source_target_pairs={{4,0},{5,1},{6,2},{7,3},{0,4},{1,5},{2,6},{3,7},{12,8},{13,9},{14,... | collective-permute-start | bytes 589832 | tf_op jit(solution)/shard_map/ppermute | solution.py:419
  21.9 1.2 %collective-permute-start.5 = (f32[384,128]{1,0:T(8,128)S(1)}, f32[384,128]{1,0:T(8,128)S(1)}, u32[]{:S(2)}, u32[]{:S(2)}) collective-permute-start(f32[384,128]{1,0:T(8,128)S(1)} %shard_map.49.a0), channel_id=1, source_target_pairs={{2,0},{3,1},{4,2},{5,3},{6,4},{7,5},{0,6},{1,7},{10,8},{11,9},{12,... | collective-permute-start | bytes 589832 | tf_op jit(solution)/shard_map/ppermute | solution.py:419
  23.0 2.7 %collective-permute-start.12 = (f32[384,128]{1,0:T(8,128)S(1)}, f32[384,128]{1,0:T(8,128)S(1)}, u32[]{:S(2)}, u32[]{:S(2)}) collective-permute-start(f32[384,128]{1,0:T(8,128)S(1)} %collective-permute-done.11.refs_3_), channel_id=1, source_target_pairs={{0,112},{8,120},{16,0},{24,8},{32,16},{40,24},{48,32},{56,40},{64,... | collective-permute-start | bytes 589832 | tf_op jit(solution)/shard_map/ppermute | solution.py:412
  25.7 2.2 %shard_map.51 = (bf16[4,256,1024]{2,1,0:T(8,128)(2,1)S(1)}, bf16[4,256,1024]{2,1,0:T(8,128)(2,1)S(1)}) custom-call(s32[16,128]{1,0:T(8,128)S(1)} %shard_map.46.index, f32[384,128]{1,0:T(8,128)S(1)} %collective-permute-done.refs_0_, f32[384,128]{1,0:T(8,128)S(1)} %collective-permute-done.1.refs_1_, f32[384,128]{1,0:T(8,128)S(1)} %collective-permute-done.8.refs_2_, ...), custom_call_target="tpu_custom_call" | custom-call | bytes 4194304 | tf_op jit(solution)/shard_map/pallas_call | solution.py:326
  27.9 1.1 %shard_map.50.left = bf16[256,2048]{1,0:T(8,128)(2,1)S(1)} custom-call(s32[16,128]{1,0:T(8,128)S(1)} %shard_map.46.index, f32[384,128]{1,0:T(8,128)S(1)} %shard_map.49.a0, f32[384,128]{1,0:T(8,128)S(1)} %collective-permute-done.5.a1, f32[384,128]{1,0:T(8,128)S(1)} %collective-permute-done.6.a2, f32[384,128]{1,0:T(8,128)S(1)} %collective-permute-done.7.a3), custom_call_target="tpu_custom_call" | custom-call | bytes 65536 | tf_op jit(solution)/shard_map/pallas_call | solution.py:314
  29.2 2.9 %collective-permute-start.13 = (f32[192,128]{1,0:T(8,128)S(1)}, f32[192,128]{1,0:T(8,128)S(1)}, u32[]{:S(2)}, u32[]{:S(2)}) collective-permute-start(f32[192,128]{1,0:T(8,128)S(1)} %slice.9), channel_id=1, source_target_pairs={{0,112},{8,120},{16,0},{24,8},{32,16},{40,24},{48,32},{56,40},{64,... | collective-permute-start | bytes 294920 | tf_op jit(solution)/shard_map/ppermute | solution.py:412
  32.1 2.6 %shard_map.52.total = f32[128,1024]{1,0:T(8,128)S(1)} custom-call(s32[16,128]{1,0:T(8,128)S(1)} %shard_map.46.index, bf16[256,2048]{1,0:T(8,128)(2,1)S(1)} %shard_map.50.left, bf16[1,256,1024]{2,1,0:T(8,128)(2,1)S(1)} %get-tuple-element.28.refs_0_, bf16[1,256,1024]{2,1,0:T(8,128)(2,1)S(1)} %get-tuple-element.29.refs_1_, ...), custom_call_target="tpu_custom_call" | custom-call | flops 1409286144 | bytes 1048576 | tf_op jit(solution)/shard_map/pallas_call | solution.py:347
  34.7 1.1 %shard_map.54 = f32[128,512]{1,0:T(8,128)S(1)} custom-call(s32[16,128]{1,0:T(8,128)S(1)} %shard_map.46.index, bf16[256,2048]{1,0:T(8,128)(2,1)S(1)} %shard_map.50.left, f32[192,128]{1,0:T(8,128)S(1)} %collective-permute-done.10.share0.refs_6_, f32[192,128]{1,0:T(8,128)S(1)} %collective-permute-done.13.share1.refs_7_, f32[128,1024]{1,0:T(8,128)S(1)} %shard_map.52.total), custom_call_target="tpu_custom_call" | custom-call | flops 100663296 | bytes 262144 | tf_op jit(solution)/shard_map/pallas_call | solution.py:364
  35.9 5.5 %collective-permute-start.14 = (f32[128,512]{1,0:T(8,128)S(1)}, f32[128,512]{1,0:T(8,128)S(1)}, u32[]{:S(2)}, u32[]{:S(2)}) collective-permute-start(f32[128,512]{1,0:T(8,128)S(1)} %shard_map.54), channel_id=1, source_target_pairs={{0,128},{128,0},{1,129},{129,1},{2,130},{130,2},{3,131},{131,3},{4... | collective-permute-start | bytes 786440 | tf_op jit(solution)/shard_map/ppermute | solution.py:433
  41.3 1.1 %shard_map.53 = f32[128,512]{1,0:T(8,128)S(1)} custom-call(s32[16,128]{1,0:T(8,128)S(1)} %shard_map.46.index, bf16[256,2048]{1,0:T(8,128)(2,1)S(1)} %shard_map.50.left, f32[192,128]{1,0:T(8,128)S(1)} %collective-permute-done.10.share0.refs_6_, f32[192,128]{1,0:T(8,128)S(1)} %collective-permute-done.13.share1.refs_7_, f32[128,1024]{1,0:T(8,128)S(1)} %shard_map.52.total), custom_call_target="tpu_custom_call" | custom-call | flops 100663296 | bytes 262144 | tf_op jit(solution)/shard_map/pallas_call | solution.py:364
  42.7 1.1 %shard_map.55.left = bf16[256,2048]{1,0:T(8,128)(2,1)S(1)} custom-call(s32[16,128]{1,0:T(8,128)S(1)} %shard_map.46.index, f32[384,128]{1,0:T(8,128)S(1)} %shard_map.49.a0, f32[384,128]{1,0:T(8,128)S(1)} %collective-permute-done.5.a1, f32[384,128]{1,0:T(8,128)S(1)} %collective-permute-done.6.a2, f32[384,128]{1,0:T(8,128)S(1)} %collective-permute-done.7.a3), custom_call_target="tpu_custom_call" | custom-call | bytes 65536 | tf_op jit(solution)/shard_map/pallas_call | solution.py:314
  43.8 3.3 %shard_map.56.mine = f32[128,1024]{1,0:T(8,128)S(1)} custom-call(s32[16,128]{1,0:T(8,128)S(1)} %shard_map.46.index, bf16[256,2048]{1,0:T(8,128)(2,1)S(1)} %shard_map.55.left, bf16[1,256,1024]{2,1,0:T(8,128)(2,1)S(1)} %get-tuple-element.28.refs_0_, bf16[1,256,1024]{2,1,0:T(8,128)(2,1)S(1)} %get-tuple-element.29.refs_1_, ...), custom_call_target="tpu_custom_call" | custom-call | flops 1610612736 | bytes 1048576 | tf_op jit(solution)/shard_map/pallas_call | solution.py:347
  47.7 2.4 %collective-permute-done.16.other = f32[128,512]{1,0:T(8,128)S(1)} collective-permute-done((f32[128,512]{1,0:T(8,128)S(1)}, f32[128,512]{1,0:T(8,128)S(1)}, u32[]{:S(2)}, u32[]{:S(2)}) %collective-permute-start.16) | collective-permute-done | bytes 262176 | tf_op jit(solution)/shard_map/ppermute | solution.py:436
  50.2 1.2 %collective-permute-start.17 = (f32[128,512]{1,0:T(8,128)S(1)}, f32[128,512]{1,0:T(8,128)S(1)}, u32[]{:S(2)}, u32[]{:S(2)}) collective-permute-start(f32[128,512]{1,0:T(8,128)S(1)} %collective-permute-done.16.other), channel_id=1, source_target_pairs={{0,128},{128,0},{1,129},{129,1},{2,130},{130,2},{3,131},{131,3},{4... | collective-permute-start | bytes 786440 | tf_op jit(solution)/shard_map/ppermute | solution.py:441
  51.4 1.2 %collective-permute-done.17.rest = f32[128,512]{1,0:T(8,128)S(1)} collective-permute-done((f32[128,512]{1,0:T(8,128)S(1)}, f32[128,512]{1,0:T(8,128)S(1)}, u32[]{:S(2)}, u32[]{:S(2)}) %collective-permute-start.17) | collective-permute-done | bytes 262176 | tf_op jit(solution)/shard_map/ppermute | solution.py:441
  52.5 0.9 %shard_map.57 = f32[128,1024]{1,0:T(8,128)} custom-call(f32[128,1024]{1,0:T(8,128)S(1)} %shard_map.56.mine, f32[128,1024]{1,0:T(8,128)S(1)} %collective-permute-done.15.theirs, f32[128,512]{1,0:T(8,128)S(1)} %collective-permute-done.16.other, f32[128,512]{1,0:T(8,128)S(1)} %collective-permute-done.17.rest), custom_call_target="tpu_custom_call" | custom-call | bytes 2097152 | tf_op jit(solution)/shard_map/pallas_call | solution.py:388
  (27 shorter events, 1.6 us)
Async XLA Ops:
  1.6 13.7 %collective-permute-start.1 = (f32[384,128]{1,0:T(8,128)S(1)}, f32[384,128]{1,0:T(8,128)S(1)}, u32[]{:S(2)}, u32[]{:S(2)}) collective-permute-start(f32[384,128]{1,0:T(8,128)S(1)} %get-tuple-element.20.refs_0_), channel_id=1, source_target_pairs={{0,112},{8,120},{16,0},{24,8},{32,16},{40,24},{48,32},{56,40},{64,... | collective-permute-start | bytes 589832 | tf_op jit(solution)/shard_map/ppermute | solution.py:412
  8.1 7.2 %collective-permute-start = (f32[384,128]{1,0:T(8,128)S(1)}, f32[384,128]{1,0:T(8,128)S(1)}, u32[]{:S(2)}, u32[]{:S(2)}) collective-permute-start(f32[384,128]{1,0:T(8,128)S(1)} %get-tuple-element.20.refs_0_), channel_id=1, source_target_pairs={{0,16},{8,24},{16,32},{24,40},{32,48},{40,56},{48,64},{56,72},{64,... | collective-permute-start | bytes 589832 | tf_op jit(solution)/shard_map/ppermute | solution.py:412
  8.1 6.0 %collective-permute-start.4 = (f32[96,128]{1,0:T(8,128)S(1)}, f32[96,128]{1,0:T(8,128)S(1)}, u32[]{:S(2)}, u32[]{:S(2)}) collective-permute-start(f32[96,128]{1,0:T(8,128)S(1)} %get-tuple-element.19.refs_0_), channel_id=1, source_target_pairs={{0,9},{1,8},{2,11},{3,10},{4,13},{5,12},{6,15},{7,14},{8,1},{9,0},... | collective-permute-start | bytes 147464 | tf_op jit(solution)/shard_map/ppermute | solution.py:414
  10.8 4.4 %collective-permute-start.3 = (f32[96,128]{1,0:T(8,128)S(1)}, f32[96,128]{1,0:T(8,128)S(1)}, u32[]{:S(2)}, u32[]{:S(2)}) collective-permute-start(f32[96,128]{1,0:T(8,128)S(1)} %get-tuple-element.19.refs_0_), channel_id=1, source_target_pairs={{0,1},{1,0},{2,3},{3,2},{4,5},{5,4},{6,7},{7,6},{8,9},{9,8},{10,11... | collective-permute-start | bytes 147464 | tf_op jit(solution)/shard_map/ppermute | solution.py:414
  11.2 4.1 %collective-permute-start.2 = (f32[96,128]{1,0:T(8,128)S(1)}, f32[96,128]{1,0:T(8,128)S(1)}, u32[]{:S(2)}, u32[]{:S(2)}) collective-permute-start(f32[96,128]{1,0:T(8,128)S(1)} %get-tuple-element.19.refs_0_), channel_id=1, source_target_pairs={{0,8},{1,9},{2,10},{3,11},{4,12},{5,13},{6,14},{7,15},{8,0},{9,1},... | collective-permute-start | bytes 147464 | tf_op jit(solution)/shard_map/ppermute | solution.py:414
  15.3 7.8 %collective-permute-start.8 = (f32[384,128]{1,0:T(8,128)S(1)}, f32[384,128]{1,0:T(8,128)S(1)}, u32[]{:S(2)}, u32[]{:S(2)}) collective-permute-start(f32[384,128]{1,0:T(8,128)S(1)} %collective-permute-done.refs_0_), channel_id=1, source_target_pairs={{0,16},{8,24},{16,32},{24,40},{32,48},{40,56},{48,64},{56,72},{64,... | collective-permute-start | bytes 589832 | tf_op jit(solution)/shard_map/ppermute | solution.py:412
  15.4 7.7 %collective-permute-start.11 = (f32[384,128]{1,0:T(8,128)S(1)}, f32[384,128]{1,0:T(8,128)S(1)}, u32[]{:S(2)}, u32[]{:S(2)}) collective-permute-start(f32[384,128]{1,0:T(8,128)S(1)} %collective-permute-done.1.refs_1_), channel_id=1, source_target_pairs={{0,112},{8,120},{16,0},{24,8},{32,16},{40,24},{48,32},{56,40},{64,... | collective-permute-start | bytes 589832 | tf_op jit(solution)/shard_map/ppermute | solution.py:412
  18.1 9.7 %collective-permute-start.7 = (f32[384,128]{1,0:T(8,128)S(1)}, f32[384,128]{1,0:T(8,128)S(1)}, u32[]{:S(2)}, u32[]{:S(2)}) collective-permute-start(f32[384,128]{1,0:T(8,128)S(1)} %shard_map.49.a0), channel_id=1, source_target_pairs={{6,0},{7,1},{0,2},{1,3},{2,4},{3,5},{4,6},{5,7},{14,8},{15,9},{8,1... | collective-permute-start | bytes 589832 | tf_op jit(solution)/shard_map/ppermute | solution.py:419
  19.4 8.5 %collective-permute-start.6 = (f32[384,128]{1,0:T(8,128)S(1)}, f32[384,128]{1,0:T(8,128)S(1)}, u32[]{:S(2)}, u32[]{:S(2)}) collective-permute-start(f32[384,128]{1,0:T(8,128)S(1)} %shard_map.49.a0), channel_id=1, source_target_pairs={{4,0},{5,1},{6,2},{7,3},{0,4},{1,5},{2,6},{3,7},{12,8},{13,9},{14,... | collective-permute-start | bytes 589832 | tf_op jit(solution)/shard_map/ppermute | solution.py:419
  21.9 6.0 %collective-permute-start.5 = (f32[384,128]{1,0:T(8,128)S(1)}, f32[384,128]{1,0:T(8,128)S(1)}, u32[]{:S(2)}, u32[]{:S(2)}) collective-permute-start(f32[384,128]{1,0:T(8,128)S(1)} %shard_map.49.a0), channel_id=1, source_target_pairs={{2,0},{3,1},{4,2},{5,3},{6,4},{7,5},{0,6},{1,7},{10,8},{11,9},{12,... | collective-permute-start | bytes 589832 | tf_op jit(solution)/shard_map/ppermute | solution.py:419
  23.0 6.0 %collective-permute-start.9 = (f32[384,128]{1,0:T(8,128)S(1)}, f32[384,128]{1,0:T(8,128)S(1)}, u32[]{:S(2)}, u32[]{:S(2)}) collective-permute-start(f32[384,128]{1,0:T(8,128)S(1)} %collective-permute-done.8.refs_2_), channel_id=1, source_target_pairs={{0,16},{8,24},{16,32},{24,40},{32,48},{40,56},{48,64},{56,72},{64,... | collective-permute-start | bytes 589832 | tf_op jit(solution)/shard_map/ppermute | solution.py:412
  23.0 6.1 %collective-permute-start.12 = (f32[384,128]{1,0:T(8,128)S(1)}, f32[384,128]{1,0:T(8,128)S(1)}, u32[]{:S(2)}, u32[]{:S(2)}) collective-permute-start(f32[384,128]{1,0:T(8,128)S(1)} %collective-permute-done.11.refs_3_), channel_id=1, source_target_pairs={{0,112},{8,120},{16,0},{24,8},{32,16},{40,24},{48,32},{56,40},{64,... | collective-permute-start | bytes 589832 | tf_op jit(solution)/shard_map/ppermute | solution.py:412
  29.1 5.7 %collective-permute-start.10 = (f32[192,128]{1,0:T(8,128)S(1)}, f32[192,128]{1,0:T(8,128)S(1)}, u32[]{:S(2)}, u32[]{:S(2)}) collective-permute-start(f32[192,128]{1,0:T(8,128)S(1)} %slice.8), channel_id=1, source_target_pairs={{0,16},{8,24},{16,32},{24,40},{32,48},{40,56},{48,64},{56,72},{64,... | collective-permute-start | bytes 294920 | tf_op jit(solution)/shard_map/ppermute | solution.py:412
  29.2 5.6 %collective-permute-start.13 = (f32[192,128]{1,0:T(8,128)S(1)}, f32[192,128]{1,0:T(8,128)S(1)}, u32[]{:S(2)}, u32[]{:S(2)}) collective-permute-start(f32[192,128]{1,0:T(8,128)S(1)} %slice.9), channel_id=1, source_target_pairs={{0,112},{8,120},{16,0},{24,8},{32,16},{40,24},{48,32},{56,40},{64,... | collective-permute-start | bytes 294920 | tf_op jit(solution)/shard_map/ppermute | solution.py:412
  35.9 6.6 %collective-permute-start.14 = (f32[128,512]{1,0:T(8,128)S(1)}, f32[128,512]{1,0:T(8,128)S(1)}, u32[]{:S(2)}, u32[]{:S(2)}) collective-permute-start(f32[128,512]{1,0:T(8,128)S(1)} %shard_map.54), channel_id=1, source_target_pairs={{0,128},{128,0},{1,129},{129,1},{2,130},{130,2},{3,131},{131,3},{4... | collective-permute-start | bytes 786440 | tf_op jit(solution)/shard_map/ppermute | solution.py:433
  42.5 7.6 %collective-permute-start.16 = (f32[128,512]{1,0:T(8,128)S(1)}, f32[128,512]{1,0:T(8,128)S(1)}, u32[]{:S(2)}, u32[]{:S(2)}) collective-permute-start(f32[128,512]{1,0:T(8,128)S(1)} %add.3), channel_id=1, source_target_pairs={{0,8},{8,0},{16,24},{24,16},{32,40},{40,32},{48,56},{56,48},{64,72... | collective-permute-start | bytes 786440 | tf_op jit(solution)/shard_map/ppermute | solution.py:436
  47.1 5.4 %collective-permute-start.15 = (f32[128,1024]{1,0:T(8,128)S(1)}, f32[128,1024]{1,0:T(8,128)S(1)}, u32[]{:S(2)}, u32[]{:S(2)}) collective-permute-start(f32[128,1024]{1,0:T(8,128)S(1)} %shard_map.56.mine), channel_id=1, source_target_pairs={{0,128},{128,0},{1,129},{129,1},{2,130},{130,2},{3,131},{131,3},{4... | collective-permute-start | bytes 1572872 | tf_op jit(solution)/shard_map/ppermute | solution.py:440
  50.2 2.4 %collective-permute-start.17 = (f32[128,512]{1,0:T(8,128)S(1)}, f32[128,512]{1,0:T(8,128)S(1)}, u32[]{:S(2)}, u32[]{:S(2)}) collective-permute-start(f32[128,512]{1,0:T(8,128)S(1)} %collective-permute-done.16.other), channel_id=1, source_target_pairs={{0,128},{128,0},{1,129},{129,1},{2,130},{130,2},{3,131},{131,3},{4... | collective-permute-start | bytes 786440 | tf_op jit(solution)/shard_map/ppermute | solution.py:441
where the time goes:
time: 53.6 us; the launch traced here: 53.4 us
  starting transfers between devices  30.6 us (57%)
  Pallas kernels  17.8 us (33%)
  waiting for transfers between devices  4.84 us (9%)
    ppermute x8, starting transfers between devices, local(): z_send = lambda v, d: lax.ppermute(v, 'row', z_perm(d))  15 us
    pallas_call x2, Pallas kernels, call_multiply(): pl.pallas_call(kernel, out_shape=jax.ShapeDtypeStruct((128, COLS), F32),...  5.97 us
    ppermute x1, starting transfers between devices, local(): recv = lax.ppermute(give, 'layer', swap)  5.46 us
    ppermute x3, starting transfers between devices, local(): x_send = lambda v, d: lax.ppermute(v, 'col', x_perm(d))  4.89 us
    ppermute x3, starting transfers between devices, local(): lax.ppermute(left0, ('row', 'col'), near(dy, dh))  3.31 us
    pallas_call x2, Pallas kernels, call_unpack_right(): pl.pallas_call(functools.partial(unpack_right, offsets), out_shape=(jax.S...  3.23 us
    ppermute x1, waiting for transfers between devices, local(): other = lax.ppermute(send, 'row', pair)  2.41 us
    pallas_call x2, Pallas kernels, call_finish(): pl.pallas_call(functools.partial(finish, offset, keep), out_shape=jax.Sha...  2.27 us
  transfers between devices with their start and end apart: 18, of which 3 were waited for; matrix products, arithmetic and copies ran while one was open for 0% of the time, Pallas kernels for 27%

commit v1 on v0

--- a/solution.py
+++ b/solution.py
@@ -411,17 +411,18 @@
     near = lambda dy, dh: [(r * 8 + c, (r ^ dy) * 8 + (c ^ dh)) for r in range(16) for c in range(8)]
     z_send = lambda v, d: lax.ppermute(v, "row", z_perm(d))
     up1, down1 = z_send(right0, 1), z_send(right0, -1)
-    nears = [lax.ppermute(left0, ("row", "col"), near(dy, dh)) for dy, dh in ((1, 0), (0, 1), (1, 1))]
-    rights0 = call_unpack_right((0,), index, (right0,))
-    up1, down1, rights0, *nears = lax.optimization_barrier((up1, down1, rights0, *nears))
+    send_near = lambda dy, dh: lax.ppermute(left0, ("row", "col"), near(dy, dh))
+    both, over_h, over_y = send_near(1, 1), send_near(0, 1), send_near(1, 0)
+    nears = [over_y, over_h, both]
+    up1, down1, index, *nears = lax.optimization_barrier((up1, down1, index, *nears))
     left2 = call_join([left0] + nears)
     up2, down2 = z_send(up1, 1), z_send(down1, -1)
     x_send = lambda v, d: lax.ppermute(v, "col", x_perm(d))
     lefts = [left2] + [x_send(left2, d) for d in (1, 2, 3)]
     up3, down3 = z_send(up2, 1), z_send(down2, -1)
-    near_z = (-1, 1, -2, 2)
-    rights = call_unpack_right(near_z, index, (up1, down1, up2, down2))
-    ready = [((0,), rights0), (near_z, rights)]
+    near_z = (0, -1, 1, -2, 2)
+    rights = call_unpack_right(near_z, index, (right0, up1, down1, up2, down2))
+    ready = [(near_z, rights)]
     third = [(-3, (up3,)), (3, (down3,))]
     half = SLABS * BLK // 2
     far = z_send(up3[:half], 1), z_send(down3[half:], -1)

time: 53.6 us -> 53.5 us (level)
  waiting for transfers between devices: 4.84 us -> 5.74 us
  Pallas kernels: 17.8 us -> 17.1 us
    ppermute x3, waiting for transfers between devices: 1.19 us -> 2.27 us  [local(): send_near = lambda dy, dh: lax.ppermute(left0, ('row', 'col'), near(dy, dh))]
    pallas_call x2 -> x1, Pallas kernels: 3.23 us -> 2.52 us  [call_unpack_right(): pl.pallas_call(functools.partial(unpack_right, offsets), out_shape=(jax.S...]
  transfers between devices with their start and end apart: 18 -> 18, of which waited for: 3 -> 3; matrix products, arithmetic and copies ran while one was open for 0% -> 0% of each run, Pallas kernels for 27% -> 25%
where the time goes in v1:
time: 53.5 us; the launch traced here: 53.3 us
  starting transfers between devices  30.3 us (57%)
  Pallas kernels  17.1 us (32%)
  waiting for transfers between devices  5.74 us (11%)
    ppermute x8, starting transfers between devices, local(): z_send = lambda v, d: lax.ppermute(v, 'row', z_perm(d))  15 us
    pallas_call x2, Pallas kernels, call_multiply(): pl.pallas_call(kernel, out_shape=jax.ShapeDtypeStruct((128, COLS), F32),...  5.97 us
    ppermute x1, starting transfers between devices, local(): recv = lax.ppermute(give, 'layer', swap)  4.99 us
    ppermute x3, starting transfers between devices, local(): x_send = lambda v, d: lax.ppermute(v, 'col', x_perm(d))  4.89 us
    ppermute x3, starting transfers between devices, local(): send_near = lambda dy, dh: lax.ppermute(left0, ('row', 'col'), near(dy, dh))  3.31 us
    pallas_call x1, Pallas kernels, call_unpack_right(): pl.pallas_call(functools.partial(unpack_right, offsets), out_shape=(jax.S...  2.52 us
    ppermute x3, waiting for transfers between devices, local(): send_near = lambda dy, dh: lax.ppermute(left0, ('row', 'col'), near(dy, dh))  2.27 us
    pallas_call x2, Pallas kernels, call_finish(): pl.pallas_call(functools.partial(finish, offset, keep), out_shape=jax.Sha...  2.27 us
  transfers between devices with their start and end apart: 18, of which 3 were waited for; matrix products, arithmetic and copies ran while one was open for 0% of the time, Pallas kernels for 25%

profile of v1, /device:TPU:1, one launch (start us, length us, event | category | flops | bytes accessed | tf_op | source)
XLA Modules:
  0.0 53.3 jit_solution(5953219484922861451)
XLA Ops:
  0.0 1.6 %shard_map.46 = (f32[96,128]{1,0:T(8,128)S(1)}, f32[384,128]{1,0:T(8,128)S(1)}) custom-call(f32[128,512]{1,0:T(8,128)} %left_hbm.1, f32[256,1024]{1,0:T(8,128)} %right_hbm.1, s32[32,128]{1,0:T(8,128)} %left_occupied.3, s32[128,128]{1,0:T(8,128)} %right_occupied.3), custom_call_target="tpu_custom_call" | custom-call | bytes 1048576 | tf_op jit(solution)/shard_map/pallas_call | solution.py:264
  1.6 6.5 %collective-permute-start.1 = (f32[384,128]{1,0:T(8,128)S(1)}, f32[384,128]{1,0:T(8,128)S(1)}, u32[]{:S(2)}, u32[]{:S(2)}) collective-permute-start(f32[384,128]{1,0:T(8,128)S(1)} %get-tuple-element.16.refs_0_), channel_id=1, source_target_pairs={{0,112},{8,120},{16,0},{24,8},{32,16},{40,24},{48,32},{56,40},{64,... | collective-permute-start | bytes 589832 | tf_op jit(solution)/shard_map/ppermute | solution.py:412
  8.1 2.7 %collective-permute-start.4 = (f32[96,128]{1,0:T(8,128)S(1)}, f32[96,128]{1,0:T(8,128)S(1)}, u32[]{:S(2)}, u32[]{:S(2)}) collective-permute-start(f32[96,128]{1,0:T(8,128)S(1)} %get-tuple-element.17.refs_0_), channel_id=1, source_target_pairs={{0,9},{1,8},{2,11},{3,10},{4,13},{5,12},{6,15},{7,14},{8,1},{9,0},... | collective-permute-start | bytes 147464 | tf_op jit(solution)/shard_map/ppermute | solution.py:414
  11.4 1.6 %shard_map.47.index = s32[16,128]{1,0:T(8,128)S(1)} custom-call(s32[32,128]{1,0:T(8,128)} %left_occupied.3, s32[128,128]{1,0:T(8,128)} %right_occupied.3), custom_call_target="tpu_custom_call" | custom-call | bytes 262144 | tf_op jit(solution)/shard_map/pallas_call | solution.py:287
  13.0 2.3 %collective-permute-done.3.refs_2_ = f32[96,128]{1,0:T(8,128)S(1)} collective-permute-done((f32[96,128]{1,0:T(8,128)S(1)}, f32[96,128]{1,0:T(8,128)S(1)}, u32[]{:S(2)}, u32[]{:S(2)}) %collective-permute-start.3) | collective-permute-done | bytes 49184 | tf_op jit(solution)/shard_map/ppermute | solution.py:414
  15.4 2.7 %collective-permute-start.11 = (f32[384,128]{1,0:T(8,128)S(1)}, f32[384,128]{1,0:T(8,128)S(1)}, u32[]{:S(2)}, u32[]{:S(2)}) collective-permute-start(f32[384,128]{1,0:T(8,128)S(1)} %collective-permute-done.1.refs_2_), channel_id=1, source_target_pairs={{0,112},{8,120},{16,0},{24,8},{32,16},{40,24},{48,32},{56,40},{64,... | collective-permute-start | bytes 589832 | tf_op jit(solution)/shard_map/ppermute | solution.py:412
  18.1 1.3 %collective-permute-start.7 = (f32[384,128]{1,0:T(8,128)S(1)}, f32[384,128]{1,0:T(8,128)S(1)}, u32[]{:S(2)}, u32[]{:S(2)}) collective-permute-start(f32[384,128]{1,0:T(8,128)S(1)} %shard_map.48.a0), channel_id=1, source_target_pairs={{6,0},{7,1},{0,2},{1,3},{2,4},{3,5},{4,6},{5,7},{14,8},{15,9},{8,1... | collective-permute-start | bytes 589832 | tf_op jit(solution)/shard_map/ppermute | solution.py:420
  19.4 2.5 %collective-permute-start.6 = (f32[384,128]{1,0:T(8,128)S(1)}, f32[384,128]{1,0:T(8,128)S(1)}, u32[]{:S(2)}, u32[]{:S(2)}) collective-permute-start(f32[384,128]{1,0:T(8,128)S(1)} %shard_map.48.a0), channel_id=1, source_target_pairs={{4,0},{5,1},{6,2},{7,3},{0,4},{1,5},{2,6},{3,7},{12,8},{13,9},{14,... | collective-permute-start | bytes 589832 | tf_op jit(solution)/shard_map/ppermute | solution.py:420
  21.9 1.2 %collective-permute-start.5 = (f32[384,128]{1,0:T(8,128)S(1)}, f32[384,128]{1,0:T(8,128)S(1)}, u32[]{:S(2)}, u32[]{:S(2)}) collective-permute-start(f32[384,128]{1,0:T(8,128)S(1)} %shard_map.48.a0), channel_id=1, source_target_pairs={{2,0},{3,1},{4,2},{5,3},{6,4},{7,5},{0,6},{1,7},{10,8},{11,9},{12,... | collective-permute-start | bytes 589832 | tf_op jit(solution)/shard_map/ppermute | solution.py:420
  23.0 2.7 %collective-permute-start.12 = (f32[384,128]{1,0:T(8,128)S(1)}, f32[384,128]{1,0:T(8,128)S(1)}, u32[]{:S(2)}, u32[]{:S(2)}) collective-permute-start(f32[384,128]{1,0:T(8,128)S(1)} %collective-permute-done.11.refs_4_), channel_id=1, source_target_pairs={{0,112},{8,120},{16,0},{24,8},{32,16},{40,24},{48,32},{56,40},{64,... | collective-permute-start | bytes 589832 | tf_op jit(solution)/shard_map/ppermute | solution.py:412
  25.7 2.5 %shard_map.50 = (bf16[5,256,1024]{2,1,0:T(8,128)(2,1)S(1)}, bf16[5,256,1024]{2,1,0:T(8,128)(2,1)S(1)}) custom-call(s32[16,128]{1,0:T(8,128)S(1)} %shard_map.47.index, f32[384,128]{1,0:T(8,128)S(1)} %get-tuple-element.16.refs_0_, f32[384,128]{1,0:T(8,128)S(1)} %collective-permute-done.refs_1_, f32[384,128]{1,0:T(8,128)S(1)} %collective-permute-done.1.refs_2_, ...), custom_call_target="tpu_custom_call" | custom-call | bytes 5242880 | tf_op jit(solution)/shard_map/pallas_call | solution.py:326
  28.3 1.1 %shard_map.49.left = bf16[256,2048]{1,0:T(8,128)(2,1)S(1)} custom-call(s32[16,128]{1,0:T(8,128)S(1)} %shard_map.47.index, f32[384,128]{1,0:T(8,128)S(1)} %shard_map.48.a0, f32[384,128]{1,0:T(8,128)S(1)} %collective-permute-done.5.a1, f32[384,128]{1,0:T(8,128)S(1)} %collective-permute-done.6.a2, f32[384,128]{1,0:T(8,128)S(1)} %collective-permute-done.7.a3), custom_call_target="tpu_custom_call" | custom-call | bytes 65536 | tf_op jit(solution)/shard_map/pallas_call | solution.py:314
  29.5 2.9 %collective-permute-start.13 = (f32[192,128]{1,0:T(8,128)S(1)}, f32[192,128]{1,0:T(8,128)S(1)}, u32[]{:S(2)}, u32[]{:S(2)}) collective-permute-start(f32[192,128]{1,0:T(8,128)S(1)} %slice.9), channel_id=1, source_target_pairs={{0,112},{8,120},{16,0},{24,8},{32,16},{40,24},{48,32},{56,40},{64,... | collective-permute-start | bytes 294920 | tf_op jit(solution)/shard_map/ppermute | solution.py:412
  32.4 2.6 %shard_map.51.total = f32[128,1024]{1,0:T(8,128)S(1)} custom-call(s32[16,128]{1,0:T(8,128)S(1)} %shard_map.47.index, bf16[256,2048]{1,0:T(8,128)(2,1)S(1)} %shard_map.49.left, bf16[5,256,1024]{2,1,0:T(8,128)(2,1)S(1)} %get-tuple-element.24.refs_0_, bf16[5,256,1024]{2,1,0:T(8,128)(2,1)S(1)} %get-tuple-element.25.refs_1_, ...), custom_call_target="tpu_custom_call" | custom-call | flops 1409286144 | bytes 1048576 | tf_op jit(solution)/shard_map/pallas_call | solution.py:347
  35.1 1.1 %shard_map.53 = f32[128,512]{1,0:T(8,128)S(1)} custom-call(s32[16,128]{1,0:T(8,128)S(1)} %shard_map.47.index, bf16[256,2048]{1,0:T(8,128)(2,1)S(1)} %shard_map.49.left, f32[192,128]{1,0:T(8,128)S(1)} %collective-permute-done.10.share0.refs_4_, f32[192,128]{1,0:T(8,128)S(1)} %collective-permute-done.13.share1.refs_5_, f32[128,1024]{1,0:T(8,128)S(1)} %shard_map.51.total), custom_call_target="tpu_custom_call" | custom-call | flops 100663296 | bytes 262144 | tf_op jit(solution)/shard_map/pallas_call | solution.py:364
  36.2 5.0 %collective-permute-start.14 = (f32[128,512]{1,0:T(8,128)S(1)}, f32[128,512]{1,0:T(8,128)S(1)}, u32[]{:S(2)}, u32[]{:S(2)}) collective-permute-start(f32[128,512]{1,0:T(8,128)S(1)} %shard_map.53), channel_id=1, source_target_pairs={{0,128},{128,0},{1,129},{129,1},{2,130},{130,2},{3,131},{131,3},{4... | collective-permute-start | bytes 786440 | tf_op jit(solution)/shard_map/ppermute | solution.py:434
  41.2 1.1 %shard_map.52 = f32[128,512]{1,0:T(8,128)S(1)} custom-call(s32[16,128]{1,0:T(8,128)S(1)} %shard_map.47.index, bf16[256,2048]{1,0:T(8,128)(2,1)S(1)} %shard_map.49.left, f32[192,128]{1,0:T(8,128)S(1)} %collective-permute-done.10.share0.refs_4_, f32[192,128]{1,0:T(8,128)S(1)} %collective-permute-done.13.share1.refs_5_, f32[128,1024]{1,0:T(8,128)S(1)} %shard_map.51.total), custom_call_target="tpu_custom_call" | custom-call | flops 100663296 | bytes 262144 | tf_op jit(solution)/shard_map/pallas_call | solution.py:364
  42.6 1.1 %shard_map.54.left = bf16[256,2048]{1,0:T(8,128)(2,1)S(1)} custom-call(s32[16,128]{1,0:T(8,128)S(1)} %shard_map.47.index, f32[384,128]{1,0:T(8,128)S(1)} %shard_map.48.a0, f32[384,128]{1,0:T(8,128)S(1)} %collective-permute-done.5.a1, f32[384,128]{1,0:T(8,128)S(1)} %collective-permute-done.6.a2, f32[384,128]{1,0:T(8,128)S(1)} %collective-permute-done.7.a3), custom_call_target="tpu_custom_call" | custom-call | bytes 65536 | tf_op jit(solution)/shard_map/pallas_call | solution.py:314
  43.7 3.3 %shard_map.55.mine = f32[128,1024]{1,0:T(8,128)S(1)} custom-call(s32[16,128]{1,0:T(8,128)S(1)} %shard_map.47.index, bf16[256,2048]{1,0:T(8,128)(2,1)S(1)} %shard_map.54.left, bf16[5,256,1024]{2,1,0:T(8,128)(2,1)S(1)} %get-tuple-element.24.refs_0_, bf16[5,256,1024]{2,1,0:T(8,128)(2,1)S(1)} %get-tuple-element.25.refs_1_, ...), custom_call_target="tpu_custom_call" | custom-call | flops 1610612736 | bytes 1048576 | tf_op jit(solution)/shard_map/pallas_call | solution.py:347
  47.1 0.7 %collective-permute-start.15 = (f32[128,1024]{1,0:T(8,128)S(1)}, f32[128,1024]{1,0:T(8,128)S(1)}, u32[]{:S(2)}, u32[]{:S(2)}) collective-permute-start(f32[128,1024]{1,0:T(8,128)S(1)} %shard_map.55.mine), channel_id=1, source_target_pairs={{0,128},{128,0},{1,129},{129,1},{2,130},{130,2},{3,131},{131,3},{4... | collective-permute-start | bytes 1572872 | tf_op jit(solution)/shard_map/ppermute | solution.py:441
  47.8 2.2 %collective-permute-done.16.other = f32[128,512]{1,0:T(8,128)S(1)} collective-permute-done((f32[128,512]{1,0:T(8,128)S(1)}, f32[128,512]{1,0:T(8,128)S(1)}, u32[]{:S(2)}, u32[]{:S(2)}) %collective-permute-start.16) | collective-permute-done | bytes 262176 | tf_op jit(solution)/shard_map/ppermute | solution.py:437
  50.0 1.2 %collective-permute-start.17 = (f32[128,512]{1,0:T(8,128)S(1)}, f32[128,512]{1,0:T(8,128)S(1)}, u32[]{:S(2)}, u32[]{:S(2)}) collective-permute-start(f32[128,512]{1,0:T(8,128)S(1)} %collective-permute-done.16.other), channel_id=1, source_target_pairs={{0,128},{128,0},{1,129},{129,1},{2,130},{130,2},{3,131},{131,3},{4... | collective-permute-start | bytes 786440 | tf_op jit(solution)/shard_map/ppermute | solution.py:442
  51.2 1.2 %collective-permute-done.17.rest = f32[128,512]{1,0:T(8,128)S(1)} collective-permute-done((f32[128,512]{1,0:T(8,128)S(1)}, f32[128,512]{1,0:T(8,128)S(1)}, u32[]{:S(2)}, u32[]{:S(2)}) %collective-permute-start.17) | collective-permute-done | bytes 262176 | tf_op jit(solution)/shard_map/ppermute | solution.py:442
  52.4 0.9 %shard_map.56 = f32[128,1024]{1,0:T(8,128)} custom-call(f32[128,1024]{1,0:T(8,128)S(1)} %shard_map.55.mine, f32[128,1024]{1,0:T(8,128)S(1)} %collective-permute-done.15.theirs, f32[128,512]{1,0:T(8,128)S(1)} %collective-permute-done.16.other, f32[128,512]{1,0:T(8,128)S(1)} %collective-permute-done.17.rest), custom_call_target="tpu_custom_call" | custom-call | bytes 2097152 | tf_op jit(solution)/shard_map/pallas_call | solution.py:388
  (26 shorter events, 1.0 us)
Async XLA Ops:
  1.6 13.7 %collective-permute-start.1 = (f32[384,128]{1,0:T(8,128)S(1)}, f32[384,128]{1,0:T(8,128)S(1)}, u32[]{:S(2)}, u32[]{:S(2)}) collective-permute-start(f32[384,128]{1,0:T(8,128)S(1)} %get-tuple-element.16.refs_0_), channel_id=1, source_target_pairs={{0,112},{8,120},{16,0},{24,8},{32,16},{40,24},{48,32},{56,40},{64,... | collective-permute-start | bytes 589832 | tf_op jit(solution)/shard_map/ppermute | solution.py:412
  8.1 7.2 %collective-permute-start = (f32[384,128]{1,0:T(8,128)S(1)}, f32[384,128]{1,0:T(8,128)S(1)}, u32[]{:S(2)}, u32[]{:S(2)}) collective-permute-start(f32[384,128]{1,0:T(8,128)S(1)} %get-tuple-element.16.refs_0_), channel_id=1, source_target_pairs={{0,16},{8,24},{16,32},{24,40},{32,48},{40,56},{48,64},{56,72},{64,... | collective-permute-start | bytes 589832 | tf_op jit(solution)/shard_map/ppermute | solution.py:412
  8.1 4.9 %collective-permute-start.4 = (f32[96,128]{1,0:T(8,128)S(1)}, f32[96,128]{1,0:T(8,128)S(1)}, u32[]{:S(2)}, u32[]{:S(2)}) collective-permute-start(f32[96,128]{1,0:T(8,128)S(1)} %get-tuple-element.17.refs_0_), channel_id=1, source_target_pairs={{0,9},{1,8},{2,11},{3,10},{4,13},{5,12},{6,15},{7,14},{8,1},{9,0},... | collective-permute-start | bytes 147464 | tf_op jit(solution)/shard_map/ppermute | solution.py:414
  10.8 4.4 %collective-permute-start.3 = (f32[96,128]{1,0:T(8,128)S(1)}, f32[96,128]{1,0:T(8,128)S(1)}, u32[]{:S(2)}, u32[]{:S(2)}) collective-permute-start(f32[96,128]{1,0:T(8,128)S(1)} %get-tuple-element.17.refs_0_), channel_id=1, source_target_pairs={{0,1},{1,0},{2,3},{3,2},{4,5},{5,4},{6,7},{7,6},{8,9},{9,8},{10,11... | collective-permute-start | bytes 147464 | tf_op jit(solution)/shard_map/ppermute | solution.py:414
  11.2 4.1 %collective-permute-start.2 = (f32[96,128]{1,0:T(8,128)S(1)}, f32[96,128]{1,0:T(8,128)S(1)}, u32[]{:S(2)}, u32[]{:S(2)}) collective-permute-start(f32[96,128]{1,0:T(8,128)S(1)} %get-tuple-element.17.refs_0_), channel_id=1, source_target_pairs={{0,8},{1,9},{2,10},{3,11},{4,12},{5,13},{6,14},{7,15},{8,0},{9,1},... | collective-permute-start | bytes 147464 | tf_op jit(solution)/shard_map/ppermute | solution.py:414
  15.3 7.8 %collective-permute-start.8 = (f32[384,128]{1,0:T(8,128)S(1)}, f32[384,128]{1,0:T(8,128)S(1)}, u32[]{:S(2)}, u32[]{:S(2)}) collective-permute-start(f32[384,128]{1,0:T(8,128)S(1)} %collective-permute-done.refs_1_), channel_id=1, source_target_pairs={{0,16},{8,24},{16,32},{24,40},{32,48},{40,56},{48,64},{56,72},{64,... | collective-permute-start | bytes 589832 | tf_op jit(solution)/shard_map/ppermute | solution.py:412
  15.4 7.7 %collective-permute-start.11 = (f32[384,128]{1,0:T(8,128)S(1)}, f32[384,128]{1,0:T(8,128)S(1)}, u32[]{:S(2)}, u32[]{:S(2)}) collective-permute-start(f32[384,128]{1,0:T(8,128)S(1)} %collective-permute-done.1.refs_2_), channel_id=1, source_target_pairs={{0,112},{8,120},{16,0},{24,8},{32,16},{40,24},{48,32},{56,40},{64,... | collective-permute-start | bytes 589832 | tf_op jit(solution)/shard_map/ppermute | solution.py:412
  18.1 10.1 %collective-permute-start.7 = (f32[384,128]{1,0:T(8,128)S(1)}, f32[384,128]{1,0:T(8,128)S(1)}, u32[]{:S(2)}, u32[]{:S(2)}) collective-permute-start(f32[384,128]{1,0:T(8,128)S(1)} %shard_map.48.a0), channel_id=1, source_target_pairs={{6,0},{7,1},{0,2},{1,3},{2,4},{3,5},{4,6},{5,7},{14,8},{15,9},{8,1... | collective-permute-start | bytes 589832 | tf_op jit(solution)/shard_map/ppermute | solution.py:420
  19.4 8.8 %collective-permute-start.6 = (f32[384,128]{1,0:T(8,128)S(1)}, f32[384,128]{1,0:T(8,128)S(1)}, u32[]{:S(2)}, u32[]{:S(2)}) collective-permute-start(f32[384,128]{1,0:T(8,128)S(1)} %shard_map.48.a0), channel_id=1, source_target_pairs={{4,0},{5,1},{6,2},{7,3},{0,4},{1,5},{2,6},{3,7},{12,8},{13,9},{14,... | collective-permute-start | bytes 589832 | tf_op jit(solution)/shard_map/ppermute | solution.py:420
  21.9 6.4 %collective-permute-start.5 = (f32[384,128]{1,0:T(8,128)S(1)}, f32[384,128]{1,0:T(8,128)S(1)}, u32[]{:S(2)}, u32[]{:S(2)}) collective-permute-start(f32[384,128]{1,0:T(8,128)S(1)} %shard_map.48.a0), channel_id=1, source_target_pairs={{2,0},{3,1},{4,2},{5,3},{6,4},{7,5},{0,6},{1,7},{10,8},{11,9},{12,... | collective-permute-start | bytes 589832 | tf_op jit(solution)/shard_map/ppermute | solution.py:420
  23.0 6.4 %collective-permute-start.9 = (f32[384,128]{1,0:T(8,128)S(1)}, f32[384,128]{1,0:T(8,128)S(1)}, u32[]{:S(2)}, u32[]{:S(2)}) collective-permute-start(f32[384,128]{1,0:T(8,128)S(1)} %collective-permute-done.8.refs_3_), channel_id=1, source_target_pairs={{0,16},{8,24},{16,32},{24,40},{32,48},{40,56},{48,64},{56,72},{64,... | collective-permute-start | bytes 589832 | tf_op jit(solution)/shard_map/ppermute | solution.py:412
  23.0 6.5 %collective-permute-start.12 = (f32[384,128]{1,0:T(8,128)S(1)}, f32[384,128]{1,0:T(8,128)S(1)}, u32[]{:S(2)}, u32[]{:S(2)}) collective-permute-start(f32[384,128]{1,0:T(8,128)S(1)} %collective-permute-done.11.refs_4_), channel_id=1, source_target_pairs={{0,112},{8,120},{16,0},{24,8},{32,16},{40,24},{48,32},{56,40},{64,... | collective-permute-start | bytes 589832 | tf_op jit(solution)/shard_map/ppermute | solution.py:412
  29.4 5.7 %collective-permute-start.10 = (f32[192,128]{1,0:T(8,128)S(1)}, f32[192,128]{1,0:T(8,128)S(1)}, u32[]{:S(2)}, u32[]{:S(2)}) collective-permute-start(f32[192,128]{1,0:T(8,128)S(1)} %slice.8), channel_id=1, source_target_pairs={{0,16},{8,24},{16,32},{24,40},{32,48},{40,56},{48,64},{56,72},{64,... | collective-permute-start | bytes 294920 | tf_op jit(solution)/shard_map/ppermute | solution.py:412
  29.5 5.6 %collective-permute-start.13 = (f32[192,128]{1,0:T(8,128)S(1)}, f32[192,128]{1,0:T(8,128)S(1)}, u32[]{:S(2)}, u32[]{:S(2)}) collective-permute-start(f32[192,128]{1,0:T(8,128)S(1)} %slice.9), channel_id=1, source_target_pairs={{0,112},{8,120},{16,0},{24,8},{32,16},{40,24},{48,32},{56,40},{64,... | collective-permute-start | bytes 294920 | tf_op jit(solution)/shard_map/ppermute | solution.py:412
  36.2 6.2 %collective-permute-start.14 = (f32[128,512]{1,0:T(8,128)S(1)}, f32[128,512]{1,0:T(8,128)S(1)}, u32[]{:S(2)}, u32[]{:S(2)}) collective-permute-start(f32[128,512]{1,0:T(8,128)S(1)} %shard_map.53), channel_id=1, source_target_pairs={{0,128},{128,0},{1,129},{129,1},{2,130},{130,2},{3,131},{131,3},{4... | collective-permute-start | bytes 786440 | tf_op jit(solution)/shard_map/ppermute | solution.py:434
  42.4 7.6 %collective-permute-start.16 = (f32[128,512]{1,0:T(8,128)S(1)}, f32[128,512]{1,0:T(8,128)S(1)}, u32[]{:S(2)}, u32[]{:S(2)}) collective-permute-start(f32[128,512]{1,0:T(8,128)S(1)} %add.3), channel_id=1, source_target_pairs={{0,8},{8,0},{16,24},{24,16},{32,40},{40,32},{48,56},{56,48},{64,72... | collective-permute-start | bytes 786440 | tf_op jit(solution)/shard_map/ppermute | solution.py:437
  47.1 5.4 %collective-permute-start.15 = (f32[128,1024]{1,0:T(8,128)S(1)}, f32[128,1024]{1,0:T(8,128)S(1)}, u32[]{:S(2)}, u32[]{:S(2)}) collective-permute-start(f32[128,1024]{1,0:T(8,128)S(1)} %shard_map.55.mine), channel_id=1, source_target_pairs={{0,128},{128,0},{1,129},{129,1},{2,130},{130,2},{3,131},{131,3},{4... | collective-permute-start | bytes 1572872 | tf_op jit(solution)/shard_map/ppermute | solution.py:441
  50.0 2.4 %collective-permute-start.17 = (f32[128,512]{1,0:T(8,128)S(1)}, f32[128,512]{1,0:T(8,128)S(1)}, u32[]{:S(2)}, u32[]{:S(2)}) collective-permute-start(f32[128,512]{1,0:T(8,128)S(1)} %collective-permute-done.16.other), channel_id=1, source_target_pairs={{0,128},{128,0},{1,129},{129,1},{2,130},{130,2},{3,131},{131,3},{4... | collective-permute-start | bytes 786440 | tf_op jit(solution)/shard_map/ppermute | solution.py:442

commit v2 on v1

--- a/solution.py
+++ b/solution.py
@@ -418,7 +418,8 @@
     left2 = call_join([left0] + nears)
     up2, down2 = z_send(up1, 1), z_send(down1, -1)
     x_send = lambda v, d: lax.ppermute(v, "col", x_perm(d))
-    lefts = [left2] + [x_send(left2, d) for d in (1, 2, 3)]
+    third_x, first_x, second_x = x_send(left2, 3), x_send(left2, 1), x_send(left2, 2)
+    lefts = [left2, first_x, second_x, third_x]
     up3, down3 = z_send(up2, 1), z_send(down2, -1)
     near_z = (0, -1, 1, -2, 2)
     rights = call_unpack_right(near_z, index, (right0, up1, down1, up2, down2))

time: 53.5 us -> 53.5 us (level)
  no operation moved by 1% of the time
where the time goes in v2:
time: 53.5 us; the launch traced here: 53.3 us
  starting transfers between devices  30.3 us (57%)
  Pallas kernels  17.1 us (32%)
  waiting for transfers between devices  5.74 us (11%)
    ppermute x8, starting transfers between devices, local(): z_send = lambda v, d: lax.ppermute(v, 'row', z_perm(d))  15 us
    pallas_call x2, Pallas kernels, call_multiply(): pl.pallas_call(kernel, out_shape=jax.ShapeDtypeStruct((128, COLS), F32),...  5.97 us
    ppermute x1, starting transfers between devices, local(): recv = lax.ppermute(give, 'layer', swap)  4.99 us
    ppermute x3, starting transfers between devices, local(): x_send = lambda v, d: lax.ppermute(v, 'col', x_perm(d))  4.89 us
    ppermute x3, starting transfers between devices, local(): send_near = lambda dy, dh: lax.ppermute(left0, ('row', 'col'), near(dy, dh))  3.31 us
    pallas_call x1, Pallas kernels, call_unpack_right(): pl.pallas_call(functools.partial(unpack_right, offsets), out_shape=(jax.S...  2.52 us
    ppermute x3, waiting for transfers between devices, local(): send_near = lambda dy, dh: lax.ppermute(left0, ('row', 'col'), near(dy, dh))  2.27 us
    pallas_call x2, Pallas kernels, call_finish(): pl.pallas_call(functools.partial(finish, offset, keep), out_shape=jax.Sha...  2.27 us
  transfers between devices with their start and end apart: 18, of which 3 were waited for; matrix products, arithmetic and copies ran while one was open for 0% of the time, Pallas kernels for 25%

profile of v2, /device:TPU:1, one launch (start us, length us, event | category | flops | bytes accessed | tf_op | source)
XLA Modules:
  0.0 53.3 jit_solution(5953219484922861451)
XLA Ops:
  0.0 1.6 %shard_map.46 = (f32[96,128]{1,0:T(8,128)S(1)}, f32[384,128]{1,0:T(8,128)S(1)}) custom-call(f32[128,512]{1,0:T(8,128)} %left_hbm.1, f32[256,1024]{1,0:T(8,128)} %right_hbm.1, s32[32,128]{1,0:T(8,128)} %left_occupied.3, s32[128,128]{1,0:T(8,128)} %right_occupied.3), custom_call_target="tpu_custom_call" | custom-call | bytes 1048576 | tf_op jit(solution)/shard_map/pallas_call | solution.py:264
  1.6 6.5 %collective-permute-start.1 = (f32[384,128]{1,0:T(8,128)S(1)}, f32[384,128]{1,0:T(8,128)S(1)}, u32[]{:S(2)}, u32[]{:S(2)}) collective-permute-start(f32[384,128]{1,0:T(8,128)S(1)} %get-tuple-element.16.refs_0_), channel_id=1, source_target_pairs={{0,112},{8,120},{16,0},{24,8},{32,16},{40,24},{48,32},{56,40},{64,... | collective-permute-start | bytes 589832 | tf_op jit(solution)/shard_map/ppermute | solution.py:412
  8.1 2.7 %collective-permute-start.4 = (f32[96,128]{1,0:T(8,128)S(1)}, f32[96,128]{1,0:T(8,128)S(1)}, u32[]{:S(2)}, u32[]{:S(2)}) collective-permute-start(f32[96,128]{1,0:T(8,128)S(1)} %get-tuple-element.17.refs_0_), channel_id=1, source_target_pairs={{0,9},{1,8},{2,11},{3,10},{4,13},{5,12},{6,15},{7,14},{8,1},{9,0},... | collective-permute-start | bytes 147464 | tf_op jit(solution)/shard_map/ppermute | solution.py:414
  11.4 1.6 %shard_map.47.index = s32[16,128]{1,0:T(8,128)S(1)} custom-call(s32[32,128]{1,0:T(8,128)} %left_occupied.3, s32[128,128]{1,0:T(8,128)} %right_occupied.3), custom_call_target="tpu_custom_call" | custom-call | bytes 262144 | tf_op jit(solution)/shard_map/pallas_call | solution.py:287
  13.0 2.3 %collective-permute-done.3.refs_2_ = f32[96,128]{1,0:T(8,128)S(1)} collective-permute-done((f32[96,128]{1,0:T(8,128)S(1)}, f32[96,128]{1,0:T(8,128)S(1)}, u32[]{:S(2)}, u32[]{:S(2)}) %collective-permute-start.3) | collective-permute-done | bytes 49184 | tf_op jit(solution)/shard_map/ppermute | solution.py:414
  15.4 2.7 %collective-permute-start.11 = (f32[384,128]{1,0:T(8,128)S(1)}, f32[384,128]{1,0:T(8,128)S(1)}, u32[]{:S(2)}, u32[]{:S(2)}) collective-permute-start(f32[384,128]{1,0:T(8,128)S(1)} %collective-permute-done.1.refs_2_), channel_id=1, source_target_pairs={{0,112},{8,120},{16,0},{24,8},{32,16},{40,24},{48,32},{56,40},{64,... | collective-permute-start | bytes 589832 | tf_op jit(solution)/shard_map/ppermute | solution.py:412
  18.1 1.3 %collective-permute-start.7 = (f32[384,128]{1,0:T(8,128)S(1)}, f32[384,128]{1,0:T(8,128)S(1)}, u32[]{:S(2)}, u32[]{:S(2)}) collective-permute-start(f32[384,128]{1,0:T(8,128)S(1)} %shard_map.48.a0), channel_id=1, source_target_pairs={{6,0},{7,1},{0,2},{1,3},{2,4},{3,5},{4,6},{5,7},{14,8},{15,9},{8,1... | collective-permute-start | bytes 589832 | tf_op jit(solution)/shard_map/ppermute | solution.py:420
  19.4 2.5 %collective-permute-start.6 = (f32[384,128]{1,0:T(8,128)S(1)}, f32[384,128]{1,0:T(8,128)S(1)}, u32[]{:S(2)}, u32[]{:S(2)}) collective-permute-start(f32[384,128]{1,0:T(8,128)S(1)} %shard_map.48.a0), channel_id=1, source_target_pairs={{4,0},{5,1},{6,2},{7,3},{0,4},{1,5},{2,6},{3,7},{12,8},{13,9},{14,... | collective-permute-start | bytes 589832 | tf_op jit(solution)/shard_map/ppermute | solution.py:420
  21.9 1.2 %collective-permute-start.5 = (f32[384,128]{1,0:T(8,128)S(1)}, f32[384,128]{1,0:T(8,128)S(1)}, u32[]{:S(2)}, u32[]{:S(2)}) collective-permute-start(f32[384,128]{1,0:T(8,128)S(1)} %shard_map.48.a0), channel_id=1, source_target_pairs={{2,0},{3,1},{4,2},{5,3},{6,4},{7,5},{0,6},{1,7},{10,8},{11,9},{12,... | collective-permute-start | bytes 589832 | tf_op jit(solution)/shard_map/ppermute | solution.py:420
  23.0 2.7 %collective-permute-start.12 = (f32[384,128]{1,0:T(8,128)S(1)}, f32[384,128]{1,0:T(8,128)S(1)}, u32[]{:S(2)}, u32[]{:S(2)}) collective-permute-start(f32[384,128]{1,0:T(8,128)S(1)} %collective-permute-done.11.refs_4_), channel_id=1, source_target_pairs={{0,112},{8,120},{16,0},{24,8},{32,16},{40,24},{48,32},{56,40},{64,... | collective-permute-start | bytes 589832 | tf_op jit(solution)/shard_map/ppermute | solution.py:412
  25.7 2.5 %shard_map.50 = (bf16[5,256,1024]{2,1,0:T(8,128)(2,1)S(1)}, bf16[5,256,1024]{2,1,0:T(8,128)(2,1)S(1)}) custom-call(s32[16,128]{1,0:T(8,128)S(1)} %shard_map.47.index, f32[384,128]{1,0:T(8,128)S(1)} %get-tuple-element.16.refs_0_, f32[384,128]{1,0:T(8,128)S(1)} %collective-permute-done.refs_1_, f32[384,128]{1,0:T(8,128)S(1)} %collective-permute-done.1.refs_2_, ...), custom_call_target="tpu_custom_call" | custom-call | bytes 5242880 | tf_op jit(solution)/shard_map/pallas_call | solution.py:326
  28.3 1.1 %shard_map.49.left = bf16[256,2048]{1,0:T(8,128)(2,1)S(1)} custom-call(s32[16,128]{1,0:T(8,128)S(1)} %shard_map.47.index, f32[384,128]{1,0:T(8,128)S(1)} %shard_map.48.a0, f32[384,128]{1,0:T(8,128)S(1)} %collective-permute-done.5.a1, f32[384,128]{1,0:T(8,128)S(1)} %collective-permute-done.6.a2, f32[384,128]{1,0:T(8,128)S(1)} %collective-permute-done.7.a3), custom_call_target="tpu_custom_call" | custom-call | bytes 65536 | tf_op jit(solution)/shard_map/pallas_call | solution.py:314
  29.5 2.9 %collective-permute-start.13 = (f32[192,128]{1,0:T(8,128)S(1)}, f32[192,128]{1,0:T(8,128)S(1)}, u32[]{:S(2)}, u32[]{:S(2)}) collective-permute-start(f32[192,128]{1,0:T(8,128)S(1)} %slice.9), channel_id=1, source_target_pairs={{0,112},{8,120},{16,0},{24,8},{32,16},{40,24},{48,32},{56,40},{64,... | collective-permute-start | bytes 294920 | tf_op jit(solution)/shard_map/ppermute | solution.py:412
  32.4 2.6 %shard_map.51.total = f32[128,1024]{1,0:T(8,128)S(1)} custom-call(s32[16,128]{1,0:T(8,128)S(1)} %shard_map.47.index, bf16[256,2048]{1,0:T(8,128)(2,1)S(1)} %shard_map.49.left, bf16[5,256,1024]{2,1,0:T(8,128)(2,1)S(1)} %get-tuple-element.24.refs_0_, bf16[5,256,1024]{2,1,0:T(8,128)(2,1)S(1)} %get-tuple-element.25.refs_1_, ...), custom_call_target="tpu_custom_call" | custom-call | flops 1409286144 | bytes 1048576 | tf_op jit(solution)/shard_map/pallas_call | solution.py:347
  35.1 1.1 %shard_map.53 = f32[128,512]{1,0:T(8,128)S(1)} custom-call(s32[16,128]{1,0:T(8,128)S(1)} %shard_map.47.index, bf16[256,2048]{1,0:T(8,128)(2,1)S(1)} %shard_map.49.left, f32[192,128]{1,0:T(8,128)S(1)} %collective-permute-done.10.share0.refs_4_, f32[192,128]{1,0:T(8,128)S(1)} %collective-permute-done.13.share1.refs_5_, f32[128,1024]{1,0:T(8,128)S(1)} %shard_map.51.total), custom_call_target="tpu_custom_call" | custom-call | flops 100663296 | bytes 262144 | tf_op jit(solution)/shard_map/pallas_call | solution.py:364
  36.2 5.0 %collective-permute-start.14 = (f32[128,512]{1,0:T(8,128)S(1)}, f32[128,512]{1,0:T(8,128)S(1)}, u32[]{:S(2)}, u32[]{:S(2)}) collective-permute-start(f32[128,512]{1,0:T(8,128)S(1)} %shard_map.53), channel_id=1, source_target_pairs={{0,128},{128,0},{1,129},{129,1},{2,130},{130,2},{3,131},{131,3},{4... | collective-permute-start | bytes 786440 | tf_op jit(solution)/shard_map/ppermute | solution.py:435
  41.2 1.1 %shard_map.52 = f32[128,512]{1,0:T(8,128)S(1)} custom-call(s32[16,128]{1,0:T(8,128)S(1)} %shard_map.47.index, bf16[256,2048]{1,0:T(8,128)(2,1)S(1)} %shard_map.49.left, f32[192,128]{1,0:T(8,128)S(1)} %collective-permute-done.10.share0.refs_4_, f32[192,128]{1,0:T(8,128)S(1)} %collective-permute-done.13.share1.refs_5_, f32[128,1024]{1,0:T(8,128)S(1)} %shard_map.51.total), custom_call_target="tpu_custom_call" | custom-call | flops 100663296 | bytes 262144 | tf_op jit(solution)/shard_map/pallas_call | solution.py:364
  42.6 1.1 %shard_map.54.left = bf16[256,2048]{1,0:T(8,128)(2,1)S(1)} custom-call(s32[16,128]{1,0:T(8,128)S(1)} %shard_map.47.index, f32[384,128]{1,0:T(8,128)S(1)} %shard_map.48.a0, f32[384,128]{1,0:T(8,128)S(1)} %collective-permute-done.5.a1, f32[384,128]{1,0:T(8,128)S(1)} %collective-permute-done.6.a2, f32[384,128]{1,0:T(8,128)S(1)} %collective-permute-done.7.a3), custom_call_target="tpu_custom_call" | custom-call | bytes 65536 | tf_op jit(solution)/shard_map/pallas_call | solution.py:314
  43.7 3.3 %shard_map.55.mine = f32[128,1024]{1,0:T(8,128)S(1)} custom-call(s32[16,128]{1,0:T(8,128)S(1)} %shard_map.47.index, bf16[256,2048]{1,0:T(8,128)(2,1)S(1)} %shard_map.54.left, bf16[5,256,1024]{2,1,0:T(8,128)(2,1)S(1)} %get-tuple-element.24.refs_0_, bf16[5,256,1024]{2,1,0:T(8,128)(2,1)S(1)} %get-tuple-element.25.refs_1_, ...), custom_call_target="tpu_custom_call" | custom-call | flops 1610612736 | bytes 1048576 | tf_op jit(solution)/shard_map/pallas_call | solution.py:347
  47.1 0.7 %collective-permute-start.15 = (f32[128,1024]{1,0:T(8,128)S(1)}, f32[128,1024]{1,0:T(8,128)S(1)}, u32[]{:S(2)}, u32[]{:S(2)}) collective-permute-start(f32[128,1024]{1,0:T(8,128)S(1)} %shard_map.55.mine), channel_id=1, source_target_pairs={{0,128},{128,0},{1,129},{129,1},{2,130},{130,2},{3,131},{131,3},{4... | collective-permute-start | bytes 1572872 | tf_op jit(solution)/shard_map/ppermute | solution.py:442
  47.8 2.2 %collective-permute-done.16.other = f32[128,512]{1,0:T(8,128)S(1)} collective-permute-done((f32[128,512]{1,0:T(8,128)S(1)}, f32[128,512]{1,0:T(8,128)S(1)}, u32[]{:S(2)}, u32[]{:S(2)}) %collective-permute-start.16) | collective-permute-done | bytes 262176 | tf_op jit(solution)/shard_map/ppermute | solution.py:438
  50.0 1.2 %collective-permute-start.17 = (f32[128,512]{1,0:T(8,128)S(1)}, f32[128,512]{1,0:T(8,128)S(1)}, u32[]{:S(2)}, u32[]{:S(2)}) collective-permute-start(f32[128,512]{1,0:T(8,128)S(1)} %collective-permute-done.16.other), channel_id=1, source_target_pairs={{0,128},{128,0},{1,129},{129,1},{2,130},{130,2},{3,131},{131,3},{4... | collective-permute-start | bytes 786440 | tf_op jit(solution)/shard_map/ppermute | solution.py:443
  51.2 1.2 %collective-permute-done.17.rest = f32[128,512]{1,0:T(8,128)S(1)} collective-permute-done((f32[128,512]{1,0:T(8,128)S(1)}, f32[128,512]{1,0:T(8,128)S(1)}, u32[]{:S(2)}, u32[]{:S(2)}) %collective-permute-start.17) | collective-permute-done | bytes 262176 | tf_op jit(solution)/shard_map/ppermute | solution.py:443
  52.4 0.9 %shard_map.56 = f32[128,1024]{1,0:T(8,128)} custom-call(f32[128,1024]{1,0:T(8,128)S(1)} %shard_map.55.mine, f32[128,1024]{1,0:T(8,128)S(1)} %collective-permute-done.15.theirs, f32[128,512]{1,0:T(8,128)S(1)} %collective-permute-done.16.other, f32[128,512]{1,0:T(8,128)S(1)} %collective-permute-done.17.rest), custom_call_target="tpu_custom_call" | custom-call | bytes 2097152 | tf_op jit(solution)/shard_map/pallas_call | solution.py:388
  (26 shorter events, 1.0 us)
Async XLA Ops:
  1.6 13.7 %collective-permute-start.1 = (f32[384,128]{1,0:T(8,128)S(1)}, f32[384,128]{1,0:T(8,128)S(1)}, u32[]{:S(2)}, u32[]{:S(2)}) collective-permute-start(f32[384,128]{1,0:T(8,128)S(1)} %get-tuple-element.16.refs_0_), channel_id=1, source_target_pairs={{0,112},{8,120},{16,0},{24,8},{32,16},{40,24},{48,32},{56,40},{64,... | collective-permute-start | bytes 589832 | tf_op jit(solution)/shard_map/ppermute | solution.py:412
  8.1 7.2 %collective-permute-start = (f32[384,128]{1,0:T(8,128)S(1)}, f32[384,128]{1,0:T(8,128)S(1)}, u32[]{:S(2)}, u32[]{:S(2)}) collective-permute-start(f32[384,128]{1,0:T(8,128)S(1)} %get-tuple-element.16.refs_0_), channel_id=1, source_target_pairs={{0,16},{8,24},{16,32},{24,40},{32,48},{40,56},{48,64},{56,72},{64,... | collective-permute-start | bytes 589832 | tf_op jit(solution)/shard_map/ppermute | solution.py:412
  8.1 4.9 %collective-permute-start.4 = (f32[96,128]{1,0:T(8,128)S(1)}, f32[96,128]{1,0:T(8,128)S(1)}, u32[]{:S(2)}, u32[]{:S(2)}) collective-permute-start(f32[96,128]{1,0:T(8,128)S(1)} %get-tuple-element.17.refs_0_), channel_id=1, source_target_pairs={{0,9},{1,8},{2,11},{3,10},{4,13},{5,12},{6,15},{7,14},{8,1},{9,0},... | collective-permute-start | bytes 147464 | tf_op jit(solution)/shard_map/ppermute | solution.py:414
  10.8 4.4 %collective-permute-start.3 = (f32[96,128]{1,0:T(8,128)S(1)}, f32[96,128]{1,0:T(8,128)S(1)}, u32[]{:S(2)}, u32[]{:S(2)}) collective-permute-start(f32[96,128]{1,0:T(8,128)S(1)} %get-tuple-element.17.refs_0_), channel_id=1, source_target_pairs={{0,1},{1,0},{2,3},{3,2},{4,5},{5,4},{6,7},{7,6},{8,9},{9,8},{10,11... | collective-permute-start | bytes 147464 | tf_op jit(solution)/shard_map/ppermute | solution.py:414
  11.2 4.1 %collective-permute-start.2 = (f32[96,128]{1,0:T(8,128)S(1)}, f32[96,128]{1,0:T(8,128)S(1)}, u32[]{:S(2)}, u32[]{:S(2)}) collective-permute-start(f32[96,128]{1,0:T(8,128)S(1)} %get-tuple-element.17.refs_0_), channel_id=1, source_target_pairs={{0,8},{1,9},{2,10},{3,11},{4,12},{5,13},{6,14},{7,15},{8,0},{9,1},... | collective-permute-start | bytes 147464 | tf_op jit(solution)/shard_map/ppermute | solution.py:414
  15.3 7.8 %collective-permute-start.8 = (f32[384,128]{1,0:T(8,128)S(1)}, f32[384,128]{1,0:T(8,128)S(1)}, u32[]{:S(2)}, u32[]{:S(2)}) collective-permute-start(f32[384,128]{1,0:T(8,128)S(1)} %collective-permute-done.refs_1_), channel_id=1, source_target_pairs={{0,16},{8,24},{16,32},{24,40},{32,48},{40,56},{48,64},{56,72},{64,... | collective-permute-start | bytes 589832 | tf_op jit(solution)/shard_map/ppermute | solution.py:412
  15.4 7.7 %collective-permute-start.11 = (f32[384,128]{1,0:T(8,128)S(1)}, f32[384,128]{1,0:T(8,128)S(1)}, u32[]{:S(2)}, u32[]{:S(2)}) collective-permute-start(f32[384,128]{1,0:T(8,128)S(1)} %collective-permute-done.1.refs_2_), channel_id=1, source_target_pairs={{0,112},{8,120},{16,0},{24,8},{32,16},{40,24},{48,32},{56,40},{64,... | collective-permute-start | bytes 589832 | tf_op jit(solution)/shard_map/ppermute | solution.py:412
  18.1 10.1 %collective-permute-start.7 = (f32[384,128]{1,0:T(8,128)S(1)}, f32[384,128]{1,0:T(8,128)S(1)}, u32[]{:S(2)}, u32[]{:S(2)}) collective-permute-start(f32[384,128]{1,0:T(8,128)S(1)} %shard_map.48.a0), channel_id=1, source_target_pairs={{6,0},{7,1},{0,2},{1,3},{2,4},{3,5},{4,6},{5,7},{14,8},{15,9},{8,1... | collective-permute-start | bytes 589832 | tf_op jit(solution)/shard_map/ppermute | solution.py:420
  19.4 8.8 %collective-permute-start.6 = (f32[384,128]{1,0:T(8,128)S(1)}, f32[384,128]{1,0:T(8,128)S(1)}, u32[]{:S(2)}, u32[]{:S(2)}) collective-permute-start(f32[384,128]{1,0:T(8,128)S(1)} %shard_map.48.a0), channel_id=1, source_target_pairs={{4,0},{5,1},{6,2},{7,3},{0,4},{1,5},{2,6},{3,7},{12,8},{13,9},{14,... | collective-permute-start | bytes 589832 | tf_op jit(solution)/shard_map/ppermute | solution.py:420
  21.9 6.4 %collective-permute-start.5 = (f32[384,128]{1,0:T(8,128)S(1)}, f32[384,128]{1,0:T(8,128)S(1)}, u32[]{:S(2)}, u32[]{:S(2)}) collective-permute-start(f32[384,128]{1,0:T(8,128)S(1)} %shard_map.48.a0), channel_id=1, source_target_pairs={{2,0},{3,1},{4,2},{5,3},{6,4},{7,5},{0,6},{1,7},{10,8},{11,9},{12,... | collective-permute-start | bytes 589832 | tf_op jit(solution)/shard_map/ppermute | solution.py:420
  23.0 6.4 %collective-permute-start.9 = (f32[384,128]{1,0:T(8,128)S(1)}, f32[384,128]{1,0:T(8,128)S(1)}, u32[]{:S(2)}, u32[]{:S(2)}) collective-permute-start(f32[384,128]{1,0:T(8,128)S(1)} %collective-permute-done.8.refs_3_), channel_id=1, source_target_pairs={{0,16},{8,24},{16,32},{24,40},{32,48},{40,56},{48,64},{56,72},{64,... | collective-permute-start | bytes 589832 | tf_op jit(solution)/shard_map/ppermute | solution.py:412
  23.0 6.5 %collective-permute-start.12 = (f32[384,128]{1,0:T(8,128)S(1)}, f32[384,128]{1,0:T(8,128)S(1)}, u32[]{:S(2)}, u32[]{:S(2)}) collective-permute-start(f32[384,128]{1,0:T(8,128)S(1)} %collective-permute-done.11.refs_4_), channel_id=1, source_target_pairs={{0,112},{8,120},{16,0},{24,8},{32,16},{40,24},{48,32},{56,40},{64,... | collective-permute-start | bytes 589832 | tf_op jit(solution)/shard_map/ppermute | solution.py:412
  29.4 5.7 %collective-permute-start.10 = (f32[192,128]{1,0:T(8,128)S(1)}, f32[192,128]{1,0:T(8,128)S(1)}, u32[]{:S(2)}, u32[]{:S(2)}) collective-permute-start(f32[192,128]{1,0:T(8,128)S(1)} %slice.8), channel_id=1, source_target_pairs={{0,16},{8,24},{16,32},{24,40},{32,48},{40,56},{48,64},{56,72},{64,... | collective-permute-start | bytes 294920 | tf_op jit(solution)/shard_map/ppermute | solution.py:412
  29.5 5.6 %collective-permute-start.13 = (f32[192,128]{1,0:T(8,128)S(1)}, f32[192,128]{1,0:T(8,128)S(1)}, u32[]{:S(2)}, u32[]{:S(2)}) collective-permute-start(f32[192,128]{1,0:T(8,128)S(1)} %slice.9), channel_id=1, source_target_pairs={{0,112},{8,120},{16,0},{24,8},{32,16},{40,24},{48,32},{56,40},{64,... | collective-permute-start | bytes 294920 | tf_op jit(solution)/shard_map/ppermute | solution.py:412
  36.2 6.2 %collective-permute-start.14 = (f32[128,512]{1,0:T(8,128)S(1)}, f32[128,512]{1,0:T(8,128)S(1)}, u32[]{:S(2)}, u32[]{:S(2)}) collective-permute-start(f32[128,512]{1,0:T(8,128)S(1)} %shard_map.53), channel_id=1, source_target_pairs={{0,128},{128,0},{1,129},{129,1},{2,130},{130,2},{3,131},{131,3},{4... | collective-permute-start | bytes 786440 | tf_op jit(solution)/shard_map/ppermute | solution.py:435
  42.4 7.6 %collective-permute-start.16 = (f32[128,512]{1,0:T(8,128)S(1)}, f32[128,512]{1,0:T(8,128)S(1)}, u32[]{:S(2)}, u32[]{:S(2)}) collective-permute-start(f32[128,512]{1,0:T(8,128)S(1)} %add.3), channel_id=1, source_target_pairs={{0,8},{8,0},{16,24},{24,16},{32,40},{40,32},{48,56},{56,48},{64,72... | collective-permute-start | bytes 786440 | tf_op jit(solution)/shard_map/ppermute | solution.py:438
  47.1 5.4 %collective-permute-start.15 = (f32[128,1024]{1,0:T(8,128)S(1)}, f32[128,1024]{1,0:T(8,128)S(1)}, u32[]{:S(2)}, u32[]{:S(2)}) collective-permute-start(f32[128,1024]{1,0:T(8,128)S(1)} %shard_map.55.mine), channel_id=1, source_target_pairs={{0,128},{128,0},{1,129},{129,1},{2,130},{130,2},{3,131},{131,3},{4... | collective-permute-start | bytes 1572872 | tf_op jit(solution)/shard_map/ppermute | solution.py:442
  50.0 2.4 %collective-permute-start.17 = (f32[128,512]{1,0:T(8,128)S(1)}, f32[128,512]{1,0:T(8,128)S(1)}, u32[]{:S(2)}, u32[]{:S(2)}) collective-permute-start(f32[128,512]{1,0:T(8,128)S(1)} %collective-permute-done.16.other), channel_id=1, source_target_pairs={{0,128},{128,0},{1,129},{129,1},{2,130},{130,2},{3,131},{131,3},{4... | collective-permute-start | bytes 786440 | tf_op jit(solution)/shard_map/ppermute | solution.py:443
